TPU v7x, 256 devices: a whole 4x4x8 slice. The times are simulated.
256 devices in a mesh: grp: 8 (over y, core), dev: 32 (over x, z).
Axes of the slice: x: 4, y: 4, z: 8, core: 2. Of those that a mesh axis runs over, the one named last changes fastest.
Arguments:
- velocity: float32 [3, 512, 65536], P(None, None, ('grp', 'dev'))
- density: float32 [512, 65536], P(None, ('grp', 'dev')), may hold values from 0.1 to 3
- inverse_density: float32 [512, 65536], P(None, ('grp', 'dev')), may hold values from 0.25 to 4
- neighbours: int32 [6, 65536], P(None, ('grp', 'dev')), may hold values from -1 to 65535, as said below
- leaf_layer: int32 [65536], P(('grp', 'dev')), may hold values from 0 to 63, as said below
- leaf_tile: int32 [65536, 1], P(('grp', 'dev')), may hold values from 0 to 31; in each aligned block of 256 rows (0 to 255, 256 to 511, ...) at most 16 rows name the same one
- leaf_block: int32 [65536], P(('grp', 'dev')), may hold values from 0 to 255
- samples: int32 [32], replicated, may hold values from 1 to 64
Outputs:
- projected_velocity: float32 [3, 512, 65536], P(None, None, ('grp', 'dev'))
- rendered: float32 [32, 16384], P('dev', 'grp')
Inputs may be any that keep to these rules, and one draw needn't show every extreme that they name: `neighbours`: A neighbour in direction -x or +x lies on the same device or on the device with dev index one lower or higher in the same group; one in -y or +y on the same device or on the device with the same dev index in the group one lower or higher; one in -z or +z on the same device. The relation is symmetric: leaf m is beside l in direction f exactly when l is beside m in the opposite direction. A device's leaves are distinct places of a brick of 8 x 8 x 8 leaf places. `leaf_layer`: the layer of a leaf of group g lies in g * 8 to g * 8 + 7. `leaf_tile`: among the 256 leaves of one device, no tile is named by more than 16, a bound that some block reaches.
All inputs are finite; a program needn't handle non-finite values.
Results may differ from a plain program's by a relative error of at most 0.0001.
Values sent between devices are 32-bit elements; how exact they have to be, the bound alone decides.
A program may use at most 64 MiB of HBM per device.

v0:
```python
import jax
import jax.numpy as jnp
from jax import lax
from jax.sharding import PartitionSpec as P

ITERS = 3
BLOCKS = 256


advect_step = 0.2
ray_step = 0.03


def extended(block, sides, width):
    for axis, dim in sides:
        count = lax.axis_size(axis)
        forward = [(i, i + 1) for i in range(count - 1)]
        backward = [(target, source) for source, target in forward]
        low = lax.ppermute(
            lax.slice_in_dim(block, block.shape[dim] - width, None, axis=dim), axis, forward
        )
        high = lax.ppermute(lax.slice_in_dim(block, 0, width, axis=dim), axis, backward)
        block = jnp.concatenate([low, block, high], axis=dim)
    return block


def shifted(first, second, third, face_list):
    leaf_count = first.shape[-1]
    minus_x = jnp.concatenate([face_list[0].reshape(1, 8, 8, leaf_count), first[:-1]], axis=0)
    plus_x = jnp.concatenate([first[1:], face_list[1].reshape(1, 8, 8, leaf_count)], axis=0)
    minus_y = jnp.concatenate([face_list[2].reshape(8, 1, 8, leaf_count), second[:, :-1]], axis=1)
    plus_y = jnp.concatenate([second[:, 1:], face_list[3].reshape(8, 1, 8, leaf_count)], axis=1)
    minus_z = jnp.concatenate([face_list[4].reshape(8, 8, 1, leaf_count), third[:, :, :-1]], axis=2)
    plus_z = jnp.concatenate([third[:, :, 1:], face_list[5].reshape(8, 8, 1, leaf_count)], axis=2)
    return [minus_x, plus_x, minus_y, plus_y, minus_z, plus_z]


def energy_sum(residual, precond):
    return lax.psum(jnp.sum(residual * precond), ("grp", "dev"))


def blend_faces(base_list, factor, added_list):
    return [base_list[face_id] + factor * added_list[face_id] for face_id in range(6)]


def shards(
    velocity, density, inverse_density, neighbours, leaf_layer, leaf_tile, leaf_block, samples
):
    leaf_count = density.shape[1]
    members = lax.axis_size("dev")
    myself = lax.axis_index("grp") * members + lax.axis_index("dev")
    owner_id = neighbours // leaf_count
    slot_index = neighbours % leaf_count
    present = neighbours >= 0
    lookup = jnp.where(
        present, jnp.where(owner_id == myself, slot_index, slot_index + leaf_count), 0
    )
    grid_shape = (8, 8, 8, leaf_count)

    def face_values(first, second, third):
        x_stack = jnp.stack([first[0].reshape(64, leaf_count), first[7].reshape(64, leaf_count)])
        x_rim = extended(x_stack, (("dev", 0),), 1)
        y_stack = jnp.stack(
            [second[:, 0].reshape(64, leaf_count), second[:, 7].reshape(64, leaf_count)]
        )
        y_rim = extended(y_stack, (("grp", 0),), 1)
        tables = [
            jnp.concatenate([x_stack[1], x_rim[0]], axis=1),
            jnp.concatenate([x_stack[0], x_rim[3]], axis=1),
            jnp.concatenate([y_stack[1], y_rim[0]], axis=1),
            jnp.concatenate([y_stack[0], y_rim[3]], axis=1),
            third[:, :, 7].reshape(64, leaf_count),
            third[:, :, 0].reshape(64, leaf_count),
        ]
        return [
            jnp.where(
                present[face_id][None, :], jnp.take(tables[face_id], lookup[face_id], axis=1), 0.0
            )
            for face_id in range(6)
        ]

    def beside_all(first, second, third):
        return shifted(first, second, third, face_values(first, second, third))

    inverse = inverse_density.reshape(grid_shape)
    dens_grid = density.reshape(grid_shape)
    velocity_grid = velocity.reshape((3,) + grid_shape)
    ones_grid = jnp.ones(grid_shape, jnp.float32)
    presence_faces = [
        jnp.broadcast_to(present[face_id][None, :].astype(jnp.float32), (64, leaf_count))
        for face_id in range(6)
    ]
    presence = shifted(ones_grid, ones_grid, ones_grid, presence_faces)
    inverse_near = beside_all(inverse, inverse, inverse)
    coupling = [
        0.5 * (inverse + inverse_near[face_id]) + 0.5 * inverse * (1.0 - presence[face_id])
        for face_id in range(6)
    ]
    diagonal = coupling[0] + coupling[1] + coupling[2] + coupling[3] + coupling[4] + coupling[5]
    vel_near = beside_all(velocity_grid[0], velocity_grid[1], velocity_grid[2])
    source = -0.5 * (
        vel_near[1] - vel_near[0] + (vel_near[3] - vel_near[2]) + (vel_near[5] - vel_near[4])
    )
    pressure = jnp.zeros(grid_shape, jnp.float32)
    press_faces = [jnp.zeros((64, leaf_count), jnp.float32) for face_id in range(6)]
    residual = source
    precond = residual / diagonal
    energy = energy_sum(residual, precond)
    direction = precond
    for iteration in range(ITERS):
        face_list = face_values(direction, direction, direction)
        near_list = shifted(direction, direction, direction, face_list)
        total = diagonal * direction
        for operate_face_id in range(6):
            total = total - coupling[operate_face_id] * near_list[operate_face_id]
        curvature = lax.psum(jnp.sum(direction * total), ("grp", "dev"))
        step_size = energy / curvature
        pressure = pressure + step_size * direction
        press_faces = blend_faces(press_faces, step_size, face_list)
        residual = residual - step_size * total
        if iteration + 1 < ITERS:
            precond = residual / diagonal
            fresh = energy_sum(residual, precond)
            direction = precond + fresh / energy * direction
            energy = fresh
    press_near = beside_all(pressure, pressure, pressure)
    gradient = (
        jnp.stack(
            [
                press_near[1] - press_near[0],
                press_near[3] - press_near[2],
                press_near[5] - press_near[4],
            ]
        )
        * 0.5
    )
    new_velocity = velocity_grid - inverse[None] * gradient
    flux = dens_grid[None] * new_velocity
    flux_near = beside_all(flux[0], flux[1], flux[2])
    change = 0.5 * (
        flux_near[1] - flux_near[0] + (flux_near[3] - flux_near[2]) + (flux_near[5] - flux_near[4])
    )
    advected = dens_grid - advect_step * change
    column = ray_step * jnp.sum(advected, axis=1).reshape(64, leaf_count)
    tile_count = samples.shape[0]
    tile_ids = leaf_tile[:, 0]
    tile_hot = (tile_ids[:, None] == jnp.arange(tile_count, dtype=jnp.int32)[None, :]).astype(
        jnp.int32
    )
    march_limit = jnp.sum(tile_hot * samples[None, :], axis=1)
    marched = (leaf_layer < march_limit).astype(jnp.float32)
    contrib = column * marched[None, :]
    target_cell = tile_ids * BLOCKS + leaf_block
    block_hot = (
        target_cell[:, None] == jnp.arange(tile_count * BLOCKS, dtype=jnp.int32)[None, :]
    ).astype(jnp.float32)
    full_image = jnp.dot(
        contrib, block_hot, precision=lax.Precision.HIGHEST, preferred_element_type=jnp.float32
    )
    partial_value = lax.psum_scatter(
        full_image.reshape(64, tile_count, BLOCKS), "dev", scatter_dimension=1, tiled=True
    )[:, 0, :]
    optical = lax.psum_scatter(partial_value, "grp", scatter_dimension=0, tiled=True)
    rendered = (1.0 - jnp.exp(-optical)).reshape(1, -1)
    return (new_velocity.reshape(3, 512, leaf_count), rendered)


def solution(mesh):
    return jax.shard_map(
        shards,
        mesh=mesh,
        in_specs=(
            P(None, None, ("grp", "dev")),
            P(None, ("grp", "dev")),
            P(None, ("grp", "dev")),
            P(None, ("grp", "dev")),
            P(("grp", "dev")),
            P(("grp", "dev"), None),
            P(("grp", "dev")),
            P(),
        ),
        out_specs=(P(None, None, ("grp", "dev")), P("dev", "grp")),
        check_vma=False,
    )
```

profile of v0, /device:TPU:1, one launch (start us, length us, event | category | flops | bytes accessed | tf_op | source)
XLA Modules:
  0.0 974.1 jit_solution(12175136879393473730)
XLA Ops:
  8.9 5.3 collective-permute-start.7
  19.5 3.6 collective-permute-start.6
  72.9 4.6 fusion.56
  83.3 5.4 collective-permute-start.8
  91.5 4.5 collective-permute-start.10
  128.2 4.5 multiply_reduce_fusion.3
  132.7 81.2 %all-reduce.6 = (f32[]{:T(128)}, f32[]{:T(128)}) all-reduce(f32[]{:T(128)} %get-tuple-element.5, f32[]{:T(128)} %get-tuple-element.4), channel_id=1, replica_groups=mesh['grp'=8,'dev'=32] {'grp','dev'}, use_global_device_ids=true, to_apply=%region_1.4 | all-reduce | flops 2 | bytes 16 | tf_op jit(solution)/shard_map/psum | solution.py:39
  218.0 73.5 %psum.44 = f32[]{:T(128)} all-reduce(f32[]{:T(128)} %get-tuple-element.16), channel_id=1, replica_groups=mesh['grp'=8,'dev'=32] {'grp','dev'}, use_global_device_ids=true, to_apply=%region_5.8 | all-reduce | flops 1 | bytes 8 | tf_op jit(solution)/shard_map/psum | solution.py:39
  299.7 3.4 collective-permute-start.12
  305.9 3.5 collective-permute-start.14
  341.6 4.4 multiply_reduce_fusion.1
  346.0 75.5 %psum.45 = f32[]{:T(128)} all-reduce(f32[]{:T(128)} %get-tuple-element.14), channel_id=1, replica_groups=mesh['grp'=8,'dev'=32] {'grp','dev'}, use_global_device_ids=true, to_apply=%region_7.10 | all-reduce | flops 1 | bytes 8 | tf_op jit(solution)/shard_map/psum | solution.py:116
  425.4 74.2 %psum.46 = f32[]{:T(128)} all-reduce(f32[]{:T(128)} %multiply_reduce_fusion), channel_id=1, replica_groups=mesh['grp'=8,'dev'=32] {'grp','dev'}, use_global_device_ids=true, to_apply=%region_9.12 | all-reduce | flops 1 | bytes 8 | tf_op jit(solution)/shard_map/psum | solution.py:39
  508.1 3.5 collective-permute-start.16
  514.4 3.5 collective-permute-start.18
  550.1 3.8 fusion.46
  554.5 75.7 %psum.47 = f32[]{:T(128)} all-reduce(f32[]{:T(128)} %fusion.46), channel_id=1, replica_groups=mesh['grp'=8,'dev'=32] {'grp','dev'}, use_global_device_ids=true, to_apply=%region_11.14 | all-reduce | flops 1 | bytes 8 | tf_op jit(solution)/shard_map/psum | solution.py:116
  635.0 4.3 collective-permute-start.21
  643.1 3.6 collective-permute-start.23
  685.8 3.6 collective-permute-start.27
  696.3 5.5 collective-permute-start.25
  716.9 5.5 fusion
  723.3 206.0 %reduce-scatter.3.cloned.1.call-done = f32[64,1,256]{2,0,1:T(8,128)} async-done(((f32[64,32,256]{2,0,1:T(8,128)}), f32[64,1,256]{2,0,1:T(8,128)}) %reduce-scatter.3.cloned.1.call-update) | async-done | bytes 65552 | tf_op jit(solution)/shard_map/reduce_scatter | solution.py:160
  931.9 34.0 %reduce-scatter.5.cloned.1.call-done = f32[8,256]{1,0:T(8,128)} async-done(((f32[64,256]{1,0:T(8,128)}), f32[8,256]{1,0:T(8,128)}) %reduce-scatter.5.cloned.1.call-update) | async-done | bytes 8208 | tf_op jit(solution)/shard_map/reduce_scatter | solution.py:163
  (496 shorter events, 258.8 us)
Async XLA Ops:
  7.2 922.1 %reduce-scatter.3.cloned.1.call-start = ((), (), s32[]{:S(2)}) async-start(), calls=%async_computation.2 | async-start | bytes 2162688 | tf_op jit(solution)/shard_map/reduce_scatter | solution.py:160
  8.9 45.1 %collective-permute-start.7 = (f32[1,64,256]{1,2,0:T(8,128)}, f32[1,64,256]{1,2,0:T(8,128)}, u32[]{:S(2)}, u32[]{:S(2)}) collective-permute-start(f32[1,64,256]{1,2,0:T(8,128)} %copy.417), channel_id=1, source_target_pairs={{32,0},{64,32},{96,64},{128,96},{160,128},{192,160},{224,192},{33,... | collective-permute-start | bytes 196616 | tf_op jit(solution)/shard_map/ppermute | solution.py:22
  16.8 41.8 %collective-permute-start.2 = (f32[1,64,256]{1,2,0:T(8,128)}, f32[1,64,256]{1,2,0:T(8,128)}, u32[]{:S(2)}, u32[]{:S(2)}) collective-permute-start(f32[1,64,256]{1,2,0:T(8,128)} %copy.395), channel_id=1, source_target_pairs={{32,0},{64,32},{96,64},{128,96},{160,128},{192,160},{224,192},{33,... | collective-permute-start | bytes 196616 | tf_op jit(solution)/shard_map/ppermute | solution.py:22
  19.5 42.0 %collective-permute-start.6 = (f32[1,64,256]{1,2,0:T(8,128)}, f32[1,64,256]{1,2,0:T(8,128)}, u32[]{:S(2)}, u32[]{:S(2)}) collective-permute-start(f32[1,64,256]{1,2,0:T(8,128)} %copy.413), channel_id=1, source_target_pairs={{0,32},{32,64},{64,96},{96,128},{128,160},{160,192},{192,224},{1,3... | collective-permute-start | bytes 196616 | tf_op jit(solution)/shard_map/ppermute | solution.py:19
  23.9 40.6 %collective-permute-start.3 = (f32[1,64,256]{1,2,0:T(8,128)}, f32[1,64,256]{1,2,0:T(8,128)}, u32[]{:S(2)}, u32[]{:S(2)}) collective-permute-start(f32[1,64,256]{1,2,0:T(8,128)} %copy.399), channel_id=1, source_target_pairs={{0,32},{32,64},{64,96},{96,128},{128,160},{160,192},{192,224},{1,3... | collective-permute-start | bytes 196616 | tf_op jit(solution)/shard_map/ppermute | solution.py:19
  27.4 38.8 %collective-permute-start.1 = (f32[1,64,256]{1,2,0:T(8,128)S(1)}, f32[1,64,256]{1,2,0:T(8,128)}, u32[]{:S(2)}, u32[]{:S(2)}) collective-permute-start(f32[1,64,256]{1,2,0:T(8,128)S(1)} %copy.542), channel_id=1, source_target_pairs={{0,1},{1,2},{2,3},{3,4},{4,5},{5,6},{6,7},{7,8},{8,9},{9,10},{10,1... | collective-permute-start | bytes 196616 | tf_op jit(solution)/shard_map/ppermute | solution.py:19
  83.3 28.5 %collective-permute-start.8 = (f32[1,64,256]{1,2,0:T(8,128)}, f32[1,64,256]{1,2,0:T(8,128)}, u32[]{:S(2)}, u32[]{:S(2)}) collective-permute-start(f32[1,64,256]{1,2,0:T(8,128)} %copy.427), channel_id=1, source_target_pairs={{0,1},{1,2},{2,3},{3,4},{4,5},{5,6},{6,7},{7,8},{8,9},{9,10},{10,1... | collective-permute-start | bytes 196616 | tf_op jit(solution)/shard_map/ppermute | solution.py:19
  89.5 25.7 %collective-permute-start.9 = (f32[1,64,256]{1,2,0:T(8,128)}, f32[1,64,256]{1,2,0:T(8,128)}, u32[]{:S(2)}, u32[]{:S(2)}) collective-permute-start(f32[1,64,256]{1,2,0:T(8,128)} %copy.430), channel_id=1, source_target_pairs={{1,0},{2,1},{3,2},{4,3},{5,4},{6,5},{7,6},{8,7},{9,8},{10,9},{11,1... | collective-permute-start | bytes 196616 | tf_op jit(solution)/shard_map/ppermute | solution.py:22
  91.5 27.6 %collective-permute-start.10 = (f32[1,64,256]{1,2,0:T(8,128)}, f32[1,64,256]{1,2,0:T(8,128)}, u32[]{:S(2)}, u32[]{:S(2)}) collective-permute-start(f32[1,64,256]{1,2,0:T(8,128)} %copy.433), channel_id=1, source_target_pairs={{0,32},{32,64},{64,96},{96,128},{128,160},{160,192},{192,224},{1,3... | collective-permute-start | bytes 196616 | tf_op jit(solution)/shard_map/ppermute | solution.py:19
  96.8 28.8 %collective-permute-start.11 = (f32[1,64,256]{1,2,0:T(8,128)}, f32[1,64,256]{1,2,0:T(8,128)}, u32[]{:S(2)}, u32[]{:S(2)}) collective-permute-start(f32[1,64,256]{1,2,0:T(8,128)} %copy.437), channel_id=1, source_target_pairs={{32,0},{64,32},{96,64},{128,96},{160,128},{192,160},{224,192},{33,... | collective-permute-start | bytes 196616 | tf_op jit(solution)/shard_map/ppermute | solution.py:22
  299.7 25.5 %collective-permute-start.12 = (f32[1,64,256]{1,2,0:T(8,128)}, f32[1,64,256]{1,2,0:T(8,128)}, u32[]{:S(2)}, u32[]{:S(2)}) collective-permute-start(f32[1,64,256]{1,2,0:T(8,128)} %copy.447), channel_id=1, source_target_pairs={{0,1},{1,2},{2,3},{3,4},{4,5},{5,6},{6,7},{7,8},{8,9},{9,10},{10,1... | collective-permute-start | bytes 196616 | tf_op jit(solution)/shard_map/ppermute | solution.py:19
  303.9 24.6 %collective-permute-start.13 = (f32[1,64,256]{1,2,0:T(8,128)}, f32[1,64,256]{1,2,0:T(8,128)}, u32[]{:S(2)}, u32[]{:S(2)}) collective-permute-start(f32[1,64,256]{1,2,0:T(8,128)} %copy.450), channel_id=1, source_target_pairs={{1,0},{2,1},{3,2},{4,3},{5,4},{6,5},{7,6},{8,7},{9,8},{10,9},{11,1... | collective-permute-start | bytes 196616 | tf_op jit(solution)/shard_map/ppermute | solution.py:22
  305.9 26.6 %collective-permute-start.14 = (f32[1,64,256]{1,2,0:T(8,128)}, f32[1,64,256]{1,2,0:T(8,128)}, u32[]{:S(2)}, u32[]{:S(2)}) collective-permute-start(f32[1,64,256]{1,2,0:T(8,128)} %copy.453), channel_id=1, source_target_pairs={{0,32},{32,64},{64,96},{96,128},{128,160},{160,192},{192,224},{1,3... | collective-permute-start | bytes 196616 | tf_op jit(solution)/shard_map/ppermute | solution.py:19
  310.2 28.8 %collective-permute-start.15 = (f32[1,64,256]{1,2,0:T(8,128)}, f32[1,64,256]{1,2,0:T(8,128)}, u32[]{:S(2)}, u32[]{:S(2)}) collective-permute-start(f32[1,64,256]{1,2,0:T(8,128)} %copy.457), channel_id=1, source_target_pairs={{32,0},{64,32},{96,64},{128,96},{160,128},{192,160},{224,192},{33,... | collective-permute-start | bytes 196616 | tf_op jit(solution)/shard_map/ppermute | solution.py:22
  508.1 25.6 %collective-permute-start.16 = (f32[1,64,256]{1,2,0:T(8,128)}, f32[1,64,256]{1,2,0:T(8,128)}, u32[]{:S(2)}, u32[]{:S(2)}) collective-permute-start(f32[1,64,256]{1,2,0:T(8,128)} %copy.467), channel_id=1, source_target_pairs={{0,1},{1,2},{2,3},{3,4},{4,5},{5,6},{6,7},{7,8},{8,9},{9,10},{10,1... | collective-permute-start | bytes 196616 | tf_op jit(solution)/shard_map/ppermute | solution.py:19
  512.4 24.7 %collective-permute-start.17 = (f32[1,64,256]{1,2,0:T(8,128)}, f32[1,64,256]{1,2,0:T(8,128)}, u32[]{:S(2)}, u32[]{:S(2)}) collective-permute-start(f32[1,64,256]{1,2,0:T(8,128)} %copy.470), channel_id=1, source_target_pairs={{1,0},{2,1},{3,2},{4,3},{5,4},{6,5},{7,6},{8,7},{9,8},{10,9},{11,1... | collective-permute-start | bytes 196616 | tf_op jit(solution)/shard_map/ppermute | solution.py:22
  514.4 26.7 %collective-permute-start.18 = (f32[1,64,256]{1,2,0:T(8,128)}, f32[1,64,256]{1,2,0:T(8,128)}, u32[]{:S(2)}, u32[]{:S(2)}) collective-permute-start(f32[1,64,256]{1,2,0:T(8,128)} %copy.473), channel_id=1, source_target_pairs={{0,32},{32,64},{64,96},{96,128},{128,160},{160,192},{192,224},{1,3... | collective-permute-start | bytes 196616 | tf_op jit(solution)/shard_map/ppermute | solution.py:19
  518.7 28.8 %collective-permute-start.19 = (f32[1,64,256]{1,2,0:T(8,128)}, f32[1,64,256]{1,2,0:T(8,128)}, u32[]{:S(2)}, u32[]{:S(2)}) collective-permute-start(f32[1,64,256]{1,2,0:T(8,128)} %copy.477), channel_id=1, source_target_pairs={{32,0},{64,32},{96,64},{128,96},{160,128},{192,160},{224,192},{33,... | collective-permute-start | bytes 196616 | tf_op jit(solution)/shard_map/ppermute | solution.py:22
  635.0 18.9 %collective-permute-start.21 = (f32[1,64,256]{1,2,0:T(8,128)}, f32[1,64,256]{1,2,0:T(8,128)}, u32[]{:S(2)}, u32[]{:S(2)}) collective-permute-start(f32[1,64,256]{1,2,0:T(8,128)} %copy.490), channel_id=1, source_target_pairs={{0,1},{1,2},{2,3},{3,4},{4,5},{5,6},{6,7},{7,8},{8,9},{9,10},{10,1... | collective-permute-start | bytes 196616 | tf_op jit(solution)/shard_map/ppermute | solution.py:19
  640.1 16.2 %collective-permute-start.20 = (f32[1,64,256]{1,2,0:T(8,128)}, f32[1,64,256]{1,2,0:T(8,128)}, u32[]{:S(2)}, u32[]{:S(2)}) collective-permute-start(f32[1,64,256]{1,2,0:T(8,128)} %copy.487), channel_id=1, source_target_pairs={{1,0},{2,1},{3,2},{4,3},{5,4},{6,5},{7,6},{8,7},{9,8},{10,9},{11,1... | collective-permute-start | bytes 196616 | tf_op jit(solution)/shard_map/ppermute | solution.py:22
  676.4 25.4 %collective-permute-start.26 = (f32[1,64,256]{1,2,0:T(8,128)}, f32[1,64,256]{1,2,0:T(8,128)}, u32[]{:S(2)}, u32[]{:S(2)}) collective-permute-start(f32[1,64,256]{1,2,0:T(8,128)} %copy.513), channel_id=1, source_target_pairs={{32,0},{64,32},{96,64},{128,96},{160,128},{192,160},{224,192},{33,... | collective-permute-start | bytes 196616 | tf_op jit(solution)/shard_map/ppermute | solution.py:22
  685.8 18.5 %collective-permute-start.27 = (f32[1,64,256]{1,2,0:T(8,128)}, f32[1,64,256]{1,2,0:T(8,128)}, u32[]{:S(2)}, u32[]{:S(2)}) collective-permute-start(f32[1,64,256]{1,2,0:T(8,128)} %copy.517), channel_id=1, source_target_pairs={{0,32},{32,64},{64,96},{96,128},{128,160},{160,192},{192,224},{1,3... | collective-permute-start | bytes 196616 | tf_op jit(solution)/shard_map/ppermute | solution.py:19
  692.6 16.6 %collective-permute-start.24 = (f32[1,64,256]{1,2,0:T(8,128)}, f32[1,64,256]{1,2,0:T(8,128)}, u32[]{:S(2)}, u32[]{:S(2)}) collective-permute-start(f32[1,64,256]{1,2,0:T(8,128)} %copy.507), channel_id=1, source_target_pairs={{1,0},{2,1},{3,2},{4,3},{5,4},{6,5},{7,6},{8,7},{9,8},{10,9},{11,1... | collective-permute-start | bytes 196616 | tf_op jit(solution)/shard_map/ppermute | solution.py:22
  722.4 243.5 %reduce-scatter.5.cloned.1.call-start = ((), (), s32[]{:S(2)}) async-start(), calls=%async_computation.3 | async-start | bytes 73728 | tf_op jit(solution)/shard_map/reduce_scatter | solution.py:163
  (62 other events, 931.4 us)
Sparse Core Ops, SparseCore 0:
  722.5 206.7 reduce-scatter.2
  931.9 33.9 reduce-scatter.4
where the time goes:
time: 979 us; the launch traced here: 974 us
  blocking collectives  380 us (39%)
  waiting for transfers between devices  240 us (25%)
  local copies, waits for them, and re-layouts  155 us (16%)
  other arithmetic  93.3 us (10%)
  starting transfers between devices  77.7 us (8%)
  between operations  22.4 us (2%)
    psum x3, blocking collectives, energy_sum(): return lax.psum(jnp.sum(residual * precond), ('grp', 'dev'))  229 us
    reduce_scatter x1, waiting for transfers between devices, shards(): lax.psum_scatter(full_image.reshape(64, tile_count, BLOCKS), 'dev', scatt...  206 us
    psum x2, blocking collectives, shards(): curvature = lax.psum(jnp.sum(direction * total), ('grp', 'dev'))  151 us
    ppermute x14, starting transfers between devices, extended(): lax.ppermute(lax.slice_in_dim(block, block.shape[dim] - width, None, axis...  51.9 us
    gather x42, local copies, waits for them, and re-layouts, face_values(): jnp.take(tables[face_id], lookup[face_id], axis=1)  39.9 us
    reduce_scatter x1, waiting for transfers between devices, shards(): lax.psum_scatter(partial_value, 'grp', scatter_dimension=0, tiled=True)  34 us
    ppermute x14, starting transfers between devices, extended(): lax.ppermute(lax.slice_in_dim(block, 0, width, axis=dim), axis, backward)  25.7 us
    select_n x33, other arithmetic, face_values(): jnp.where(present[face_id][None, :], jnp.take(tables[face_id], lookup[fac...  25.5 us
  transfers between devices with their start and end apart: 30, of which 2 were waited for; matrix products, arithmetic and copies ran while one was open for 17% of the time, Pallas kernels for 0%

commit v1 on v0

v1 whole, which is shorter than its diff:
```python
import functools

import jax
import jax.numpy as jnp
from jax import lax
from jax.experimental import pallas as pl
from jax.experimental.pallas import tpu as pltpu
from jax.sharding import PartitionSpec as P

BLOCKS = 256
advect_step = 0.2
ray_step = 0.03
L = 256
FACE = 64
CAP = 16
F32 = jnp.float32
BF16 = jnp.bfloat16
MESH = pl.DeviceIdType.MESH


def parts(x):
    hi = x.astype(BF16)
    rest = x - hi.astype(F32)
    mid = rest.astype(BF16)
    low = (rest - mid.astype(F32)).astype(BF16)
    return jnp.concatenate([hi, mid, low], axis=0)


def joined(y):
    rows = y.shape[0] // 3
    return y[:rows] + y[rows : 2 * rows] + y[2 * rows :]


def pick(x, hot):
    return joined(jnp.dot(parts(x), hot, preferred_element_type=F32))


def pick_t(x, hot):
    return joined(
        lax.dot_general(parts(x), hot, (((1,), (1,)), ((), ())), preferred_element_type=F32)
    )


def spread(row, rows):
    return jnp.broadcast_to(row, (rows, row.shape[1]))


def hot_of(condition):
    return jnp.where(condition, 1.0, 0.0).astype(BF16)


def kernel(
    n_grp,
    n_dev,
    vel,
    dens,
    inv,
    nbr,
    layer,
    tile,
    block,
    samples,
    newv,
    rendered,
    wp,
    vx,
    vy,
    vz,
    dn,
    q,
    zf,
    zt,
    cs,
    dg,
    pp,
    gl,
    gr,
    cp,
    er,
    r1,
    rf,
    sb,
    rb,
    a1s,
    a1r,
    a2s,
    a2r,
    ids,
    idr,
    das,
    dar,
    ims,
    imr,
    sx,
    fy,
    sz,
    sd,
    col,
    in_sem,
    hs_sem,
    hr_sem,
    gs_sem,
    gr_sem,
    ds_sem,
    dr_sem,
):
    g = lax.axis_index("grp")
    d = lax.axis_index("dev")
    me = g * n_dev + d

    def grp_at(step):
        return (lax.rem(g + step, n_grp), d)

    def dev_at(step):
        return (g, lax.rem(d + step, n_dev))

    barrier = pltpu.get_barrier_semaphore()

    @pl.loop(1, n_dev)
    def _(i):
        pl.semaphore_signal(barrier, inc=1, device_id=dev_at(i), device_id_type=MESH)

    @pl.loop(1, n_grp)
    def _(i):
        pl.semaphore_signal(barrier, inc=1, device_id=grp_at(i), device_id_type=MESH)

    loads = [
        pltpu.make_async_copy(inv, wp.at[pl.ds(1, 8), pl.ds(1, 8)], in_sem.at[0]),
        pltpu.make_async_copy(vel.at[0], vx.at[pl.ds(1, 8)], in_sem.at[1]),
        pltpu.make_async_copy(vel.at[1], vy.at[:, pl.ds(1, 8)], in_sem.at[2]),
        pltpu.make_async_copy(vel.at[2], vz, in_sem.at[3]),
        pltpu.make_async_copy(dens, dn, in_sem.at[4]),
    ]
    for load in loads:
        load.start()

    pl.semaphore_wait(barrier, n_dev - 1 + n_grp - 1)

    to = [dev_at(1), dev_at(n_dev - 1), grp_at(1), grp_at(n_grp - 1)]

    def halo(number, face, src, dst):
        return pltpu.make_async_remote_copy(
            src_ref=src,
            dst_ref=dst,
            send_sem=hs_sem.at[number, face],
            recv_sem=hr_sem.at[number, face],
            device_id=to[face],
            device_id_type=MESH,
        )

    raw = []
    for which, field in enumerate((inv, vel, dens)):
        x_field = vel.at[0] if which == 1 else field
        y_field = vel.at[1] if which == 1 else field
        raw.append(
            [
                halo(which, 0, x_field.at[7], r1.at[0, which]),
                halo(which, 1, x_field.at[0], r1.at[1, which]),
                halo(which, 2, y_field.at[:, 7], r1.at[2, which]),
                halo(which, 3, y_field.at[:, 0], r1.at[3, which]),
            ]
        )
        for copy in raw[-1]:
            copy.start()

    table = nbr[...]
    present = table >= 0
    local = present & ((table // L) == me)
    remote = present & ((table // L) != me)
    slot = table % L
    local_slot = jnp.where(local, slot, -1)
    remote_slot = jnp.where(remote, slot, -1)
    sub = lax.broadcasted_iota(jnp.int32, (L, L), 0)
    lane = lax.broadcasted_iota(jnp.int32, (L, L), 1)
    upper = hot_of(sub < lane)
    sub128 = lax.broadcasted_iota(jnp.int32, (2 * FACE, L), 0)
    for face in range(6):
        gl[face] = hot_of(sub == spread(local_slot[face : face + 1], L))
    tile_row = tile[...]
    tile_hot = hot_of(
        lax.broadcasted_iota(jnp.int32, (n_dev, L), 0) == spread(tile_row, n_dev)
    )
    remote_hot = hot_of(remote)
    before = jnp.dot(
        jnp.concatenate([tile_hot, remote_hot, jnp.zeros((10, L), BF16)], axis=0),
        upper,
        preferred_element_type=F32,
    )
    for face in range(4):
        mine = remote_slot[face : face + 1]
        hot = jnp.where(sub == spread(mine, L), 1.0, 0.0)
        gr[face] = hot.astype(BF16)
        occupied = jnp.sum(hot, axis=1, keepdims=True)
        rank = jnp.sum(
            jnp.where(sub < spread(mine, L), occupied, 0.0), axis=0, keepdims=True
        ).astype(jnp.int32)
        rank = jnp.where(mine >= 0, rank, -1000)
        er[face, 0] = hot_of(sub128 == spread(rank, 2 * FACE))
        er[face, 1] = hot_of(sub128 == spread(rank + FACE, 2 * FACE))
        out_face = face ^ 1
        place = before[n_dev + out_face : n_dev + out_face + 1].astype(jnp.int32)
        place = jnp.where(remote_slot[out_face : out_face + 1] >= 0, place, -1000)
        cp[face, 0] = hot_of(sub128 == spread(place, 2 * FACE))
        cp[face, 1] = hot_of(sub128 == spread(place + FACE, 2 * FACE))

    rank = jnp.sum(
        jnp.where(tile_hot > 0, before[:n_dev], 0.0), axis=0, keepdims=True
    ).astype(jnp.int32)
    rows = n_dev * 8
    sub_key = lax.broadcasted_iota(jnp.int32, (rows, L), 0)
    first_key = jnp.where(rank < 8, tile_row * 8 + rank, -1)
    second_key = jnp.where(rank >= 8, tile_row * 8 + rank - 8, -1)
    slot_hot = jnp.concatenate(
        [hot_of(sub_key == spread(first_key, rows)), hot_of(sub_key == spread(second_key, rows))],
        axis=1,
    )

    def packed(values):
        zero = jnp.zeros_like(values)
        return jnp.concatenate(
            [
                jnp.concatenate([values, zero], axis=1),
                jnp.concatenate([zero, values], axis=1),
            ],
            axis=0,
        )

    def into_slots(values):
        return lax.dot_general(
            slot_hot, packed(values), (((1,), (1,)), ((), ())), preferred_element_type=F32
        )

    ids[...] = into_slots(spread(block[...], 64).astype(F32).astype(BF16)).reshape(n_dev, 8, 128)

    def to_dev(number, src, dst, i):
        return pltpu.make_async_remote_copy(
            src_ref=src,
            dst_ref=dst,
            send_sem=ds_sem.at[number, i],
            recv_sem=dr_sem.at[number, i],
            device_id=dev_at(i),
            device_id_type=MESH,
        )

    def to_grp(number, src, dst, i):
        return pltpu.make_async_remote_copy(
            src_ref=src,
            dst_ref=dst,
            send_sem=gs_sem.at[number, i],
            recv_sem=gr_sem.at[number, i],
            device_id=grp_at(i),
            device_id_type=MESH,
        )

    def ids_copy(i):
        return to_dev(0, ids.at[lax.rem(d + i, n_dev)], idr.at[i], i)

    @pl.loop(1, n_dev)
    def _(i):
        ids_copy(i).start()

    idr[0] = ids[d]
    limit = jnp.zeros((1, L), jnp.int32)
    for t in range(n_dev):
        limit = jnp.where(tile_row == t, samples[t], limit)
    marched = jnp.where(layer[...] < limit, ray_step, 0.0)

    for load in loads:
        load.wait()

    def flat(x):
        return x.reshape(FACE, L)

    def cube(x):
        return x.reshape(8, 8, L)

    def fill_z_tables(read):
        @pl.loop(0, 8)
        def _(i):
            for j in range(8):
                c = read(i, j)
                zt[0, i, j : j + 1, :] = c[7:8]
                zt[1, i, j : j + 1, :] = c[0:1]

    def local_faces(k):
        q[k, 0, 1:9] = cube(pick(flat(q[k, 8, 1:9]), gl[0]))
        q[k, 9, 1:9] = cube(pick(flat(q[k, 1, 1:9]), gl[1]))
        q[k, 1:9, 0] = cube(pick(flat(q[k, 1:9, 8]), gl[2]))
        q[k, 1:9, 9] = cube(pick(flat(q[k, 1:9, 1]), gl[3]))
        zf[2 * k] = cube(pick(flat(zt[0]), gl[4]))
        zf[2 * k + 1] = cube(pick(flat(zt[1]), gl[5]))

    fill_z_tables(lambda i, j: vz[i, j])
    zf[2] = cube(pick(flat(zt[0]), gl[4]))
    zf[3] = cube(pick(flat(zt[1]), gl[5]))
    fill_z_tables(lambda i, j: wp[i + 1, j + 1])
    absent = [jnp.where(present[face : face + 1], 0.0, 1.0) for face in range(6)]

    def both(first, second, face):
        return pick(jnp.concatenate([flat(first), flat(second)], axis=0), gl[face])

    near_local = [
        both(wp[8, 1:9], vx[8], 0),
        both(wp[1, 1:9], vx[1], 1),
        both(wp[1:9, 8], vy[:, 8], 2),
        both(wp[1:9, 1], vy[:, 1], 3),
    ]
    zf[0] = cube(pick(flat(zt[0]), gl[4]))
    zf[1] = cube(pick(flat(zt[1]), gl[5]))
    for which in range(3):
        for copy in raw[which]:
            copy.wait_recv()
    for face in range(4):
        got = pick(r1[face].reshape(3 * FACE, L), gr[face])
        rf[face] = got.reshape(3, 8, 8, L)
        near = near_local[face] + got[: 2 * FACE]
        w_near = cube(near[:FACE])
        v_near = cube(near[FACE:])
        if face == 0:
            wp[0, 1:9] = w_near + absent[face] * wp[1, 1:9]
            vx[0] = v_near
        elif face == 1:
            wp[9, 1:9] = w_near + absent[face] * wp[8, 1:9]
            vx[9] = v_near
        elif face == 2:
            wp[1:9, 0] = w_near + absent[face] * wp[1:9, 1]
            vy[:, 0] = v_near
        else:
            wp[1:9, 9] = w_near + absent[face] * wp[1:9, 8]
            vy[:, 9] = v_near

    k_id = lax.broadcasted_iota(jnp.int32, (8, L), 0)
    at_low = k_id == 0
    at_high = k_id == 7

    def beside_z(c, low, high):
        return (
            jnp.where(at_low, low, pltpu.roll(c, 1, 0)),
            jnp.where(at_high, high, pltpu.roll(c, 7, 0)),
        )

    def start_body(i, total):
        for j in range(8):
            c = wp[i + 1, j + 1]
            low, high = beside_z(
                c,
                zf[0, i, j : j + 1] + absent[4] * c[0:1],
                zf[1, i, j : j + 1] + absent[5] * c[7:8],
            )
            near = [wp[i, j + 1], wp[i + 2, j + 1], wp[i + 1, j], wp[i + 1, j + 2], low, high]
            coupling = [0.5 * (c + value) for value in near]
            diagonal = (
                coupling[0] + coupling[1] + coupling[2] + coupling[3] + coupling[4] + coupling[5]
            )
            inverse = 1.0 / diagonal
            dg[i, j] = diagonal
            for face in range(6):
                cs[face, i, j] = coupling[face] * inverse
            v = vz[i, j]
            low, high = beside_z(v, zf[2, i, j : j + 1], zf[3, i, j : j + 1])
            source = -0.5 * (
                (vx[i + 2, j] - vx[i, j]) + (vy[i, j + 2] - vy[i, j]) + (high - low)
            )
            value = source * inverse
            q[0, i + 1, j + 1] = value
            zt[0, i, j : j + 1, :] = value[7:8]
            zt[1, i, j : j + 1, :] = value[0:1]
            total = total + source * value
        return total

    zero = jnp.zeros((8, L), F32)
    moments = [lax.fori_loop(0, 8, start_body, zero)]

    def exchange(k):
        tables = [
            (flat(q[k, 8, 1:9]), flat(q[k, 7, 1:9])),
            (flat(q[k, 1, 1:9]), flat(q[k, 2, 1:9])),
            (flat(q[k, 1:9, 8]), flat(q[k, 1:9, 7])),
            (flat(q[k, 1:9, 1]), flat(q[k, 1:9, 2])),
        ]
        copies = []
        for face in range(4):
            sb[k, face] = pick_t(tables[face][0], cp[face, 0]) + pick_t(
                tables[face][1], cp[face, 1]
            )
            copies.append(halo(3 + k, face, sb.at[k, face], rb.at[k, face]))
            copies[-1].start()
        local_faces(k)
        for copy in copies:
            copy.wait_recv()
        q[k, 0, 1:9] += cube(pick(rb[k, 0], er[0, 0]))
        q[k, 9, 1:9] += cube(pick(rb[k, 1], er[1, 0]))
        q[k, 1:9, 0] += cube(pick(rb[k, 2], er[2, 0]))
        q[k, 1:9, 9] += cube(pick(rb[k, 3], er[3, 0]))
        return copies

    def apply(k):
        def body(i, totals):
            odd, even = totals
            for j in range(8):
                c = q[k, i + 1, j + 1]
                low, high = beside_z(c, zf[2 * k, i, j : j + 1], zf[2 * k + 1, i, j : j + 1])
                near = [
                    q[k, i, j + 1],
                    q[k, i + 2, j + 1],
                    q[k, i + 1, j],
                    q[k, i + 1, j + 2],
                    low,
                    high,
                ]
                value = c
                for face in range(6):
                    value = value - cs[face, i, j] * near[face]
                scaled = dg[i, j] * value
                odd = odd + c * scaled
                if k < 2:
                    even = even + value * scaled
                    q[k + 1, i + 1, j + 1] = value
                    zt[0, i, j : j + 1, :] = value[7:8]
                    zt[1, i, j : j + 1, :] = value[0:1]
            return odd, even

        return lax.fori_loop(0, 8, body, (zero, zero))

    sent = []
    for k in range(3):
        sent += exchange(k)
        odd, even = apply(k)
        moments += [odd, even]
    moments = moments[:6]

    a1s[...] = jnp.zeros((8, 128), F32)
    for k in range(6):
        line = jnp.sum(moments[k], axis=0, keepdims=True)
        a1s[k : k + 1, :] = line[:, :128] + line[:, 128:]

    for i in range(1, n_grp):
        to_grp(0, a1s, a1r.at[i], i).start()
    partial = a1s[...]
    for i in range(1, n_grp):
        to_grp(0, a1s, a1r.at[i], i).wait_recv()
        partial = partial + a1r[i]
    a2s[...] = partial

    @pl.loop(1, n_dev)
    def _(i):
        to_dev(1, a2s, a2r.at[i], i).start()

    @pl.loop(1, n_dev)
    def _(i):
        to_dev(1, a2s, a2r.at[i], i).wait_recv()

    whole = partial
    for i in range(1, n_dev):
        whole = whole + a2r[i]
    m = jnp.broadcast_to(jnp.sum(whole, axis=1, keepdims=True), (8, 128))
    m = [m[k : k + 1] for k in range(6)]
    l10 = m[2] / m[1]
    l20 = m[3] / m[1]
    d1 = m[3] - l10 * m[2]
    t21 = m[4] - l20 * m[2]
    l21 = t21 / d1
    d2 = m[5] - l20 * m[3] - l21 * t21
    y1 = m[1] - l10 * m[0]
    y2 = m[2] - l20 * m[0] - l21 * y1
    c2 = y2 / d2
    c1 = y1 / d1 - l21 * c2
    c0 = m[0] / m[1] - l10 * c1 - l20 * c2
    coefs = [jnp.concatenate([spread(c, 8), spread(c, 8)], axis=1) for c in (c0, c1, c2)]
    narrow = [spread(c, 8) for c in (c0, c1, c2)]

    def mixed(read):
        return coefs[0] * read(0) + coefs[1] * read(1) + coefs[2] * read(2)

    @pl.loop(0, 8)
    def _(i):
        pp[0, i + 1] = mixed(lambda k: q[k, 0, i + 1])
        pp[9, i + 1] = mixed(lambda k: q[k, 9, i + 1])
        zf[0, i] = mixed(lambda k: zf[2 * k, i])
        zf[1, i] = mixed(lambda k: zf[2 * k + 1, i])
        for j in range(10):
            pp[i + 1, j] = mixed(lambda k: q[k, i + 1, j])

    def far(face):
        deep = jnp.zeros((FACE, 128), F32)
        for k in range(3):
            deep = deep + jnp.broadcast_to(narrow[k][0:1], (FACE, 128)) * rb[k, face]
        deep = cube(pick(deep, er[face, 1]))
        if face == 0:
            change = pp[1, 1:9] - deep
        elif face == 1:
            change = deep - pp[8, 1:9]
        elif face == 2:
            change = pp[1:9, 1] - deep
        else:
            change = deep - pp[1:9, 8]
        return rf[face, 2] * (rf[face, 1] - 0.5 * rf[face, 0] * change)

    sx[0] = jnp.sum(far(0), axis=0)
    sx[9] = jnp.sum(far(1), axis=0)
    fy[0] = far(2)
    fy[3] = far(3)

    @pl.loop(0, 8)
    def _(i):
        sum_x = zero
        sum_z = zero
        sum_d = zero
        for j in range(8):
            c = pp[i + 1, j + 1]
            low, high = beside_z(c, zf[0, i, j : j + 1], zf[1, i, j : j + 1])
            half = 0.5 * wp[i + 1, j + 1]
            n_x = vx[i + 1, j] - half * (pp[i + 2, j + 1] - pp[i, j + 1])
            n_y = vy[i, j + 1] - half * (pp[i + 1, j + 2] - pp[i + 1, j])
            n_z = vz[i, j] - half * (high - low)
            newv[0, i, j] = n_x
            newv[1, i, j] = n_y
            newv[2, i, j] = n_z
            smoke = dn[i, j]
            sum_x = sum_x + smoke * n_x
            sum_z = sum_z + smoke * n_z
            sum_d = sum_d + smoke
            if j == 0:
                fy[1, i] = smoke * n_y
            if j == 7:
                fy[2, i] = smoke * n_y
        sx[i + 1] = sum_x
        sz[i] = sum_z
        sd[i] = sum_d
        zt[0, 0, pl.ds(i, 1), :] = sum_z[7:8]
        zt[1, 0, pl.ds(i, 1), :] = sum_z[0:1]

    fy[0] += cube(pick(flat(fy[2]), gl[2]))
    fy[3] += cube(pick(flat(fy[1]), gl[3]))
    both_x = jnp.concatenate([sx[8], sx[8]], axis=0)
    sx[0] += pick(both_x, gl[0])[:8]
    both_x = jnp.concatenate([sx[1], sx[1]], axis=0)
    sx[9] += pick(both_x, gl[1])[:8]
    z_low = pick(jnp.concatenate([zt[0, 0], zt[0, 0]], axis=0), gl[4])[:8]
    z_high = pick(jnp.concatenate([zt[1, 0], zt[1, 0]], axis=0), gl[5])[:8]
    for i in range(8):
        low, high = beside_z(sz[i], z_low[i : i + 1], z_high[i : i + 1])
        change = (
            (sx[i + 2] - sx[i]) + ((fy[3, i] + fy[2, i]) - (fy[1, i] + fy[0, i])) + (high - low)
        )
        col[8 * i : 8 * i + 8] = marched * (sd[i] - (0.5 * advect_step) * change)

    columns = parts(col[...])
    total = into_slots(columns[:64]) + into_slots(columns[64:128]) + into_slots(columns[128:])
    das[...] = total.reshape(n_dev, 8, 128)

    def data_copy(i):
        return to_dev(2, das.at[lax.rem(d + i, n_dev)], dar.at[i], i)

    @pl.loop(1, n_dev)
    def _(i):
        data_copy(i).start()

    dar[0] = das[d]

    @pl.loop(1, n_dev)
    def _(i):
        ids_copy(i).wait_recv()

    marks = idr[...].reshape(rows, 128)
    lane_b = lax.broadcasted_iota(jnp.int32, (rows, BLOCKS), 1).astype(F32)
    first_hot = hot_of(marks[:, 0:1] == lane_b)
    second_hot = hot_of(marks[:, 64:65] == lane_b)

    @pl.loop(1, n_dev)
    def _(i):
        data_copy(i).wait_recv()

    got = parts(dar[...].reshape(rows, 128).T)
    image = joined(jnp.dot(got, first_hot, preferred_element_type=F32))[:64]
    image = image + joined(jnp.dot(got, second_hot, preferred_element_type=F32))[64:]
    ims[...] = image.reshape(8, 8, BLOCKS)

    def image_copy(i):
        return to_grp(1, ims.at[lax.rem(g + i, n_grp)], imr.at[i], i)

    for i in range(1, n_grp):
        image_copy(i).start()
    optical = ims[g]
    for i in range(1, n_grp):
        image_copy(i).wait_recv()
        optical = optical + imr[i]
    shade = 1.0 - jnp.exp(-optical)
    for row in range(8):
        rendered[:, BLOCKS * row : BLOCKS * (row + 1)] = shade[row : row + 1]

    for which in range(3):
        for copy in raw[which]:
            copy.wait_send()
    for copy in sent:
        copy.wait_send()
    for i in range(1, n_grp):
        to_grp(0, a1s, a1r.at[i], i).wait_send()
        image_copy(i).wait_send()

    @pl.loop(1, n_dev)
    def _(i):
        ids_copy(i).wait_send()
        to_dev(1, a2s, a2r.at[i], i).wait_send()
        data_copy(i).wait_send()


def solution(mesh):
    n_grp, n_dev = mesh.shape["grp"], mesh.shape["dev"]

    def step(
        velocity, density, inverse_density, neighbours, leaf_layer, leaf_tile, leaf_block, samples
    ):
        vmem = pl.BlockSpec(memory_space=pltpu.VMEM)
        anywhere = pl.BlockSpec(memory_space=pl.ANY)
        smem = pl.BlockSpec(memory_space=pltpu.SMEM)
        new_velocity, rendered = pl.pallas_call(
            functools.partial(kernel, n_grp, n_dev),
            out_shape=(
                jax.ShapeDtypeStruct((3, 8, 8, 8, L), F32),
                jax.ShapeDtypeStruct((1, 8 * BLOCKS), F32),
            ),
            in_specs=[anywhere] * 3 + [vmem] * 4 + [smem],
            out_specs=(vmem, vmem),
            scratch_shapes=[
                pltpu.VMEM((10, 10, 8, L), F32),
                pltpu.VMEM((10, 8, 8, L), F32),
                pltpu.VMEM((8, 10, 8, L), F32),
                pltpu.VMEM((8, 8, 8, L), F32),
                pltpu.VMEM((8, 8, 8, L), F32),
                pltpu.VMEM((3, 10, 10, 8, L), F32),
                pltpu.VMEM((6, 8, 8, L), F32),
                pltpu.VMEM((2, 8, 8, L), F32),
                pltpu.VMEM((6, 8, 8, 8, L), F32),
                pltpu.VMEM((8, 8, 8, L), F32),
                pltpu.VMEM((10, 10, 8, L), F32),
                pltpu.VMEM((6, L, L), BF16),
                pltpu.VMEM((4, L, L), BF16),
                pltpu.VMEM((4, 2, 2 * FACE, L), BF16),
                pltpu.VMEM((4, 2, 2 * FACE, L), BF16),
                pltpu.VMEM((4, 3, 8, 8, L), F32),
                pltpu.VMEM((4, 3, 8, 8, L), F32),
                pltpu.VMEM((3, 4, FACE, 128), F32),
                pltpu.VMEM((3, 4, FACE, 128), F32),
                pltpu.VMEM((8, 128), F32),
                pltpu.VMEM((n_grp, 8, 128), F32),
                pltpu.VMEM((8, 128), F32),
                pltpu.VMEM((n_dev, 8, 128), F32),
                pltpu.VMEM((n_dev, 8, 128), F32),
                pltpu.VMEM((n_dev, 8, 128), F32),
                pltpu.VMEM((n_dev, 8, 128), F32),
                pltpu.VMEM((n_dev, 8, 128), F32),
                pltpu.VMEM((8, 8, BLOCKS), F32),
                pltpu.VMEM((n_grp, 8, BLOCKS), F32),
                pltpu.VMEM((10, 8, L), F32),
                pltpu.VMEM((4, 8, 8, L), F32),
                pltpu.VMEM((8, 8, L), F32),
                pltpu.VMEM((8, 8, L), F32),
                pltpu.VMEM((64, L), F32),
                pltpu.SemaphoreType.DMA((5,)),
                pltpu.SemaphoreType.DMA((6, 4)),
                pltpu.SemaphoreType.DMA((6, 4)),
                pltpu.SemaphoreType.DMA((2, n_grp)),
                pltpu.SemaphoreType.DMA((2, n_grp)),
                pltpu.SemaphoreType.DMA((3, n_dev)),
                pltpu.SemaphoreType.DMA((3, n_dev)),
            ],
            compiler_params=pltpu.CompilerParams(
                collective_id=0, has_side_effects=True, vmem_limit_bytes=48 * 1024 * 1024
            ),
        )(
            velocity.reshape(3, 8, 8, 8, L),
            density.reshape(8, 8, 8, L),
            inverse_density.reshape(8, 8, 8, L),
            neighbours,
            leaf_layer.reshape(1, L),
            leaf_tile.reshape(1, L),
            leaf_block.reshape(1, L),
            samples,
        )
        return new_velocity.reshape(3, 512, L), rendered

    return jax.shard_map(
        step,
        mesh=mesh,
        in_specs=(
            P(None, None, ("grp", "dev")),
            P(None, ("grp", "dev")),
            P(None, ("grp", "dev")),
            P(None, ("grp", "dev")),
            P(("grp", "dev")),
            P(("grp", "dev"), None),
            P(("grp", "dev")),
            P(),
        ),
        out_specs=(P(None, None, ("grp", "dev")), P("dev", "grp")),
        check_vma=False,
    )
```

time: 979 us -> 74.5 us (0.08)
  blocking collectives: 380 us -> 0 us
  waiting for transfers between devices: 240 us -> 0 us
  local copies, waits for them, and re-layouts: 155 us -> 8.61 us
  other arithmetic: 93.3 us -> 0 us
  starting transfers between devices: 77.7 us -> 0 us
  Pallas kernels: 0 us -> 64.9 us
  between operations: 22.4 us -> 0.66 us
    psum x5 -> x0, blocking collectives: 380 us -> none  [the longest x3 229 us: energy_sum(): return lax.psum(jnp.sum(residual * precond), ('grp', 'dev'))]
    reduce_scatter x2 -> x0, waiting for transfers between devices: 240 us -> none  [the longest x1 206 us: shards(): lax.psum_scatter(full_image.reshape(64, tile_count, BLOCKS), 'dev', scatt...]
    ppermute x28 -> x0, starting transfers between devices: 77.7 us -> none  [the longest x14 51.9 us: extended(): lax.ppermute(lax.slice_in_dim(block, block.shape[dim] - width, None, axis...]
    pallas_call x0 -> x1, Pallas kernels: none -> 64.9 us  [step(): pl.pallas_call(functools.partial(kernel, n_grp, n_dev), out_shape=(jax.Sh...]
    another operation x74 -> x0, local copies, waits for them, and re-layouts: 52.4 us -> none  [the longest x14 11.5 us: face_values(): jnp.stack([second[:, 0].reshape(64, leaf_count), second[:, 7].reshape(64,...]
    gather x42 -> x0, local copies, waits for them, and re-layouts: 39.9 us -> none  [face_values(): jnp.take(tables[face_id], lookup[face_id], axis=1)]
    select_n x40 -> x0, other arithmetic: 28.9 us -> none  [the longest x33 25.5 us: face_values(): jnp.where(present[face_id][None, :], jnp.take(tables[face_id], lookup[fac...]
    slice x30 -> x0, local copies, waits for them, and re-layouts: 26.4 us -> none  [the longest x5 5.11 us: shifted(): first[:-1]]
  transfers between devices with their start and end apart: 30 -> 0, of which waited for: 2 -> 0; matrix products, arithmetic and copies ran while one was open for 17% -> 0% of each run, Pallas kernels for 0% -> 0%
where the time goes in v1:
time: 74.5 us; the launch traced here: 74.2 us
  Pallas kernels  64.9 us (87%)
  local copies, waits for them, and re-layouts  8.61 us (12%)
    pallas_call x1, Pallas kernels, step(): pl.pallas_call(functools.partial(kernel, n_grp, n_dev), out_shape=(jax.Sh...  64.9 us
    unnamed x18, local copies, waits for them, and re-layouts  8.61 us

profile of v1, /device:TPU:1, one launch (start us, length us, event | category | flops | bytes accessed | tf_op | source)
XLA Modules:
  0.0 74.2 jit_solution(14348931785026396316)
XLA Ops:
  0.6 0.0 copy-start
  0.6 1.4 %copy-done = f32[3,512,256]{2,1,0:T(8,128)S(1)} copy-done((f32[3,512,256]{2,1,0:T(8,128)S(1)}, f32[3,512,256]{2,1,0:T(8,128)}, u32[]{:S(2)}) %copy-start) | copy-done | bytes 1572888
  2.0 0.0 copy-start.1
  2.0 1.0 %copy-done.1 = f32[512,256]{1,0:T(8,128)S(1)} copy-done((f32[512,256]{1,0:T(8,128)S(1)}, f32[512,256]{1,0:T(8,128)}, u32[]{:S(2)}) %copy-start.1) | copy-done | bytes 524312
  3.1 0.0 copy-start.2
  3.1 1.0 %copy-done.2 = f32[512,256]{1,0:T(8,128)S(1)} copy-done((f32[512,256]{1,0:T(8,128)S(1)}, f32[512,256]{1,0:T(8,128)}, u32[]{:S(2)}) %copy-start.2) | copy-done | bytes 524312
  4.1 0.0 copy-start.3
  4.1 0.7 copy-done.3
  4.8 0.0 copy-start.4
  4.8 0.7 copy-done.4
  5.5 0.0 copy-start.5
  5.5 0.7 copy-done.5
  6.2 0.0 copy-start.6
  6.2 0.7 copy-done.6
  6.9 0.0 copy-start.7
  6.9 0.7 copy-done.7
  7.5 64.9 %shard_map.95 = (f32[3,8,8,8,256]{4,3,2,1,0:T(8,128)S(1)}, f32[1,2048]{1,0:T(1,128)S(1)}) custom-call(f32[3,8,8,8,256]{4,3,2,1,0:T(8,128)S(1)} %bitcast.7, f32[8,8,8,256]{3,2,1,0:T(8,128)S(1)} %bitcast.9, f32[8,8,8,256]{3,2,1,0:T(8,128)S(1)} %bitcast.10, s32[6,256]{1,0:T(8,128)S(1)} %copy-done.3, s32[1,256]{1,0:T(1,128)S(1)} %bitcast.11, ...), custom_call_target="tpu_custom_call" | custom-call | tf_op jit(solution)/shard_map/pallas_call | solution.py:617
  72.5 1.1 %copy.12 = f32[3,512,256]{2,1,0:T(8,128)} copy(f32[3,512,256]{2,1,0:T(8,128)S(1)} %bitcast.8) | data formatting | bytes 3145728
  73.6 0.6 copy.13
Async XLA Ops:
  0.6 1.4 %copy-start = (f32[3,512,256]{2,1,0:T(8,128)S(1)}, f32[3,512,256]{2,1,0:T(8,128)}, u32[]{:S(2)}) copy-start(f32[3,512,256]{2,1,0:T(8,128)} %param.8) | copy-start | bytes 4718596
  2.0 1.0 %copy-start.1 = (f32[512,256]{1,0:T(8,128)S(1)}, f32[512,256]{1,0:T(8,128)}, u32[]{:S(2)}) copy-start(f32[512,256]{1,0:T(8,128)} %param.9) | copy-start | bytes 1572868
  3.1 1.0 %copy-start.2 = (f32[512,256]{1,0:T(8,128)S(1)}, f32[512,256]{1,0:T(8,128)}, u32[]{:S(2)}) copy-start(f32[512,256]{1,0:T(8,128)} %param.10) | copy-start | bytes 1572868
  4.1 0.7 copy-start.3
  4.8 0.7 copy-start.4
  5.5 0.7 copy-start.5
  6.2 0.7 copy-start.6
  6.9 0.7 copy-start.7

commit v2 on v1

v2 whole, which is shorter than its diff:
```python
import functools

import jax
import jax.numpy as jnp
from jax import lax
from jax.experimental import pallas as pl
from jax.experimental.pallas import tpu as pltpu
from jax.sharding import PartitionSpec as P

BLOCKS = 256
advect_step = 0.2
ray_step = 0.03
L = 256
FACE = 64
CAP = 16
F32 = jnp.float32
BF16 = jnp.bfloat16
MESH = pl.DeviceIdType.MESH


def parts(x):
    hi = x.astype(BF16)
    rest = x - hi.astype(F32)
    mid = rest.astype(BF16)
    low = (rest - mid.astype(F32)).astype(BF16)
    return jnp.concatenate([hi, mid, low], axis=0)


def joined(y):
    rows = y.shape[0] // 3
    return y[:rows] + y[rows : 2 * rows] + y[2 * rows :]


def pick(x, hot):
    return joined(jnp.dot(parts(x), hot, preferred_element_type=F32))


def pick_t(x, hot):
    return joined(
        lax.dot_general(parts(x), hot, (((1,), (1,)), ((), ())), preferred_element_type=F32)
    )


def spread(row, rows):
    return jnp.broadcast_to(row, (rows, row.shape[1]))


def hot_of(condition):
    return jnp.where(condition, 1.0, 0.0).astype(BF16)


def kernel(
    n_grp,
    n_dev,
    vel,
    dens,
    inv,
    nbr_any,
    layer_any,
    tile_any,
    block_any,
    samples,
    newv,
    rendered,
    nbr,
    rows_in,
    wp,
    vx,
    vy,
    vz,
    dn,
    hd,
    q,
    zf,
    zt,
    cs,
    dg,
    pp,
    gl,
    cp,
    er,
    rf,
    sb,
    rb,
    a1s,
    a1r,
    a2s,
    a2r,
    ids,
    idr,
    das,
    dar,
    ims,
    imr,
    sx,
    fy,
    sz,
    sd,
    col,
    in_sem,
    hs_sem,
    hr_sem,
    gs_sem,
    gr_sem,
    ds_sem,
    dr_sem,
):
    g = lax.axis_index("grp")
    d = lax.axis_index("dev")
    me = g * n_dev + d

    def grp_at(step):
        return (lax.rem(g + step, n_grp), d)

    def dev_at(step):
        return (g, lax.rem(d + step, n_dev))

    small = [
        pltpu.make_async_copy(nbr_any, nbr, in_sem.at[5]),
        pltpu.make_async_copy(tile_any, rows_in.at[0], in_sem.at[6]),
        pltpu.make_async_copy(block_any, rows_in.at[1], in_sem.at[7]),
        pltpu.make_async_copy(layer_any, rows_in.at[2], in_sem.at[8]),
    ]
    loads = [
        pltpu.make_async_copy(inv, wp.at[pl.ds(1, 8), pl.ds(1, 8)], in_sem.at[0]),
        pltpu.make_async_copy(vel.at[0], vx.at[pl.ds(1, 8)], in_sem.at[1]),
        pltpu.make_async_copy(vel.at[1], vy.at[:, pl.ds(1, 8)], in_sem.at[2]),
        pltpu.make_async_copy(dens, dn, in_sem.at[3]),
        pltpu.make_async_copy(vel.at[2], vz, in_sem.at[4]),
    ]
    for load in small + loads:
        load.start()

    to = [dev_at(1), dev_at(n_dev - 1), grp_at(1), grp_at(n_grp - 1)]
    sends = [d < n_dev - 1, d > 0, g < n_grp - 1, g > 0]
    takes = [d > 0, d < n_dev - 1, g > 0, g < n_grp - 1]

    for face in range(4):

        @pl.when(jnp.logical_not(takes[face]))
        def _():
            rb[:, face] = jnp.zeros((5, FACE, 128), F32)

    barrier = pltpu.get_barrier_semaphore()

    @pl.loop(1, n_grp)
    def _(i):
        pl.semaphore_signal(barrier, inc=1, device_id=grp_at(i), device_id_type=MESH)

    @pl.loop(1, n_dev)
    def _(i):
        pl.semaphore_signal(barrier, inc=1, device_id=dev_at(i), device_id_type=MESH)

    for load in small:
        load.wait()

    table = nbr[...]
    present = table >= 0
    local = present & ((table // L) == me)
    remote = present & ((table // L) != me)
    slot = table % L
    local_slot = jnp.where(local, slot, -1)
    remote_slot = jnp.where(remote, slot, -1)
    sub = lax.broadcasted_iota(jnp.int32, (L, L), 0)
    lane = lax.broadcasted_iota(jnp.int32, (L, L), 1)
    upper = hot_of(sub < lane)
    sub128 = lax.broadcasted_iota(jnp.int32, (2 * FACE, L), 0)
    tile_row = rows_in[0]
    tile_hot = hot_of(
        lax.broadcasted_iota(jnp.int32, (n_dev, L), 0) == spread(tile_row, n_dev)
    )
    before = jnp.dot(
        jnp.concatenate([tile_hot, hot_of(remote), jnp.zeros((10, L), BF16)], axis=0),
        upper,
        preferred_element_type=F32,
    )
    for face in range(4):
        out_face = face ^ 1
        place = before[n_dev + out_face : n_dev + out_face + 1].astype(jnp.int32)
        place = jnp.where(remote_slot[out_face : out_face + 1] >= 0, place, -1000)
        cp[face, 0] = hot_of(sub128 == spread(place, 2 * FACE))
        cp[face, 1] = hot_of(sub128 == spread(place + FACE, 2 * FACE))

    for load in loads[:4]:
        load.wait()

    def flat(x):
        return x.reshape(FACE, L)

    def cube(x):
        return x.reshape(8, 8, L)

    def halo(number, face):
        return pltpu.make_async_remote_copy(
            src_ref=sb.at[number, face],
            dst_ref=rb.at[number, face],
            send_sem=hs_sem.at[number, face],
            recv_sem=hr_sem.at[number, face],
            device_id=to[face],
            device_id_type=MESH,
        )

    def send_faces(number, first, second):
        for face in range(4):
            sb[number, face] = pick_t(flat(first[face]), cp[face, 0]) + pick_t(
                flat(second[face]), cp[face, 1]
            )

            @pl.when(sends[face])
            def _():
                halo(number, face).start()

    def take_faces(number):
        for face in range(4):

            @pl.when(takes[face])
            def _():
                halo(number, face).wait_recv()

    pl.semaphore_wait(barrier, n_dev - 1 + n_grp - 1)

    send_faces(
        3,
        [wp[8, 1:9], wp[1, 1:9], wp[1:9, 8], wp[1:9, 1]],
        [vx[8], vx[1], vy[:, 8], vy[:, 1]],
    )
    smoke_faces = [dn[7], dn[0], dn[:, 7], dn[:, 0]]
    send_faces(4, smoke_faces, smoke_faces)

    for face in range(6):
        gl[face] = hot_of(sub == spread(local_slot[face : face + 1], L))
    for face in range(4):
        mine = remote_slot[face : face + 1]
        occupied = jnp.sum(
            jnp.where(sub == spread(mine, L), 1.0, 0.0), axis=1, keepdims=True
        )
        rank = jnp.sum(
            jnp.where(sub < spread(mine, L), occupied, 0.0), axis=0, keepdims=True
        ).astype(jnp.int32)
        rank = jnp.where(mine >= 0, rank, -1000)
        er[face, 0] = hot_of(sub128 == spread(rank, 2 * FACE))
        er[face, 1] = hot_of(sub128 == spread(rank + FACE, 2 * FACE))

    rank = jnp.sum(
        jnp.where(tile_hot > 0, before[:n_dev], 0.0), axis=0, keepdims=True
    ).astype(jnp.int32)
    rows = n_dev * 8
    sub_key = lax.broadcasted_iota(jnp.int32, (rows, L), 0)
    first_key = jnp.where(rank < 8, tile_row * 8 + rank, -1)
    second_key = jnp.where(rank >= 8, tile_row * 8 + rank - 8, -1)
    slot_hot = jnp.concatenate(
        [hot_of(sub_key == spread(first_key, rows)), hot_of(sub_key == spread(second_key, rows))],
        axis=1,
    )

    def into_slots(values):
        empty = jnp.zeros_like(values)
        packed = jnp.concatenate(
            [
                jnp.concatenate([values, empty], axis=1),
                jnp.concatenate([empty, values], axis=1),
            ],
            axis=0,
        )
        return lax.dot_general(
            slot_hot, packed, (((1,), (1,)), ((), ())), preferred_element_type=F32
        )

    def to_dev(number, src, dst, i):
        return pltpu.make_async_remote_copy(
            src_ref=src,
            dst_ref=dst,
            send_sem=ds_sem.at[number, i],
            recv_sem=dr_sem.at[number, i],
            device_id=dev_at(i),
            device_id_type=MESH,
        )

    def to_grp(number, src, dst, i):
        return pltpu.make_async_remote_copy(
            src_ref=src,
            dst_ref=dst,
            send_sem=gs_sem.at[number, i],
            recv_sem=gr_sem.at[number, i],
            device_id=grp_at(i),
            device_id_type=MESH,
        )

    def ids_copy(i):
        return to_dev(0, ids.at[lax.rem(d + i, n_dev)], idr.at[i], i)

    def sum_copy(i):
        return to_dev(1, a2s, a2r.at[i], i)

    def data_copy(which, i):
        return to_dev(2 + which, das.at[which, lax.rem(d + i, n_dev)], dar.at[which, i], i)

    ids[...] = into_slots(spread(rows_in[1], 64).astype(F32).astype(BF16)).reshape(n_dev, 8, 128)

    @pl.loop(1, n_dev)
    def _(i):
        ids_copy(i).start()

    idr[0] = ids[d]
    limit = jnp.zeros((1, L), jnp.int32)
    for t in range(n_dev):
        limit = jnp.where(tile_row == t, samples[t], limit)
    marched = jnp.where(rows_in[2] < limit, ray_step, 0.0)

    loads[4].wait()

    def fill_z_tables(read):
        @pl.loop(0, 8)
        def _(i):
            for j in range(8):
                c = read(i, j)
                zt[0, i, j : j + 1, :] = c[7:8]
                zt[1, i, j : j + 1, :] = c[0:1]

    def local_faces(k):
        q[k, 0, 1:9] = cube(pick(flat(q[k, 8, 1:9]), gl[0]))
        q[k, 9, 1:9] = cube(pick(flat(q[k, 1, 1:9]), gl[1]))
        q[k, 1:9, 0] = cube(pick(flat(q[k, 1:9, 8]), gl[2]))
        q[k, 1:9, 9] = cube(pick(flat(q[k, 1:9, 1]), gl[3]))
        zf[2 * k] = cube(pick(flat(zt[0]), gl[4]))
        zf[2 * k + 1] = cube(pick(flat(zt[1]), gl[5]))

    fill_z_tables(lambda i, j: vz[i, j])
    zf[2] = cube(pick(flat(zt[0]), gl[4]))
    zf[3] = cube(pick(flat(zt[1]), gl[5]))
    fill_z_tables(lambda i, j: wp[i + 1, j + 1])
    absent = [jnp.where(present[face : face + 1], 0.0, 1.0) for face in range(6)]
    zf[0] = cube(pick(flat(zt[0]), gl[4]))
    zf[1] = cube(pick(flat(zt[1]), gl[5]))

    def both(first, second, face):
        return pick(jnp.concatenate([flat(first), flat(second)], axis=0), gl[face])

    near_local = [
        both(wp[8, 1:9], vx[8], 0),
        both(wp[1, 1:9], vx[1], 1),
        both(wp[1:9, 8], vy[:, 8], 2),
        both(wp[1:9, 1], vy[:, 1], 3),
    ]
    take_faces(3)
    for face in range(4):
        got = parts(rb[3, face])
        w_far = joined(jnp.dot(got, er[face, 0], preferred_element_type=F32))
        v_far = joined(jnp.dot(got, er[face, 1], preferred_element_type=F32))
        rf[face, 0] = cube(w_far)
        rf[face, 1] = cube(v_far)
        w_near = cube(near_local[face][:FACE] + w_far)
        v_near = cube(near_local[face][FACE:] + v_far)
        if face == 0:
            wp[0, 1:9] = w_near + absent[face] * wp[1, 1:9]
            vx[0] = v_near
        elif face == 1:
            wp[9, 1:9] = w_near + absent[face] * wp[8, 1:9]
            vx[9] = v_near
        elif face == 2:
            wp[1:9, 0] = w_near + absent[face] * wp[1:9, 1]
            vy[:, 0] = v_near
        else:
            wp[1:9, 9] = w_near + absent[face] * wp[1:9, 8]
            vy[:, 9] = v_near

    k_id = lax.broadcasted_iota(jnp.int32, (8, L), 0)
    at_low = k_id == 0
    at_high = k_id == 7
    zero = jnp.zeros((8, L), F32)

    def beside_z(c, low, high):
        return (
            jnp.where(at_low, low, pltpu.roll(c, 1, 0)),
            jnp.where(at_high, high, pltpu.roll(c, 7, 0)),
        )

    @pl.loop(0, 8)
    def _(i):
        for j in range(8):
            c = wp[i + 1, j + 1]
            low, high = beside_z(
                c,
                zf[0, i, j : j + 1] + absent[4] * c[0:1],
                zf[1, i, j : j + 1] + absent[5] * c[7:8],
            )
            near = [wp[i, j + 1], wp[i + 2, j + 1], wp[i + 1, j], wp[i + 1, j + 2], low, high]
            coupling = [0.5 * (c + value) for value in near]
            diagonal = (
                coupling[0] + coupling[1] + coupling[2] + coupling[3] + coupling[4] + coupling[5]
            )
            inverse = 1.0 / diagonal
            dg[i, j] = diagonal
            for face in range(6):
                cs[face, i, j] = coupling[face] * inverse
            v = vz[i, j]
            low, high = beside_z(v, zf[2, i, j : j + 1], zf[3, i, j : j + 1])
            source = -0.5 * (
                (vx[i + 2, j] - vx[i, j]) + (vy[i, j + 2] - vy[i, j]) + (high - low)
            )
            q[0, i + 1, j + 1] = source * inverse

    def send_field(k):
        send_faces(
            k,
            [q[k, 8, 1:9], q[k, 1, 1:9], q[k, 1:9, 8], q[k, 1:9, 1]],
            [q[k, 7, 1:9], q[k, 2, 1:9], q[k, 1:9, 7], q[k, 1:9, 2]],
        )

    send_field(0)

    def apply_local(k):
        @pl.loop(0, 8)
        def _(i):
            for j in range(8):
                c = q[k, i + 1, j + 1]
                low, high = beside_z(c, zf[2 * k, i, j : j + 1], zf[2 * k + 1, i, j : j + 1])
                near = [
                    q[k, i, j + 1],
                    q[k, i + 2, j + 1],
                    q[k, i + 1, j],
                    q[k, i + 1, j + 2],
                    low,
                    high,
                ]
                value = c
                for face in range(6):
                    value = value - cs[face, i, j] * near[face]
                q[k + 1, i + 1, j + 1] = value

    def add_far(k):
        far = [cube(pick(rb[k, face], er[face, 0])) for face in range(4)]
        q[k, 0, 1:9] += far[0]
        q[k, 9, 1:9] += far[1]
        q[k, 1:9, 0] += far[2]
        q[k, 1:9, 9] += far[3]
        q[k + 1, 1, 1:9] -= cs[0, 0] * far[0]
        q[k + 1, 8, 1:9] -= cs[1, 7] * far[1]
        q[k + 1, 1:9, 1] -= cs[2, :, 0] * far[2]
        q[k + 1, 1:9, 8] -= cs[3, :, 7] * far[3]

    def products(k):
        def body(i, totals):
            even, odd = totals
            for j in range(8):
                c = q[k, i + 1, j + 1]
                scaled = dg[i, j] * c
                even = even + c * scaled
                odd = odd + q[k + 1, i + 1, j + 1] * scaled
            return even, odd

        return lax.fori_loop(0, 8, body, (zero, zero))

    def read_z(k):
        return lambda i, j: q[k, i + 1, j + 1]

    def flux_columns(which):
        base = which == 0
        k = which - 1

        def far(face):
            if base:
                return rf[face, 2] * rf[face, 1]
            deep = cube(pick(rb[k, face], er[face, 1]))
            change = [
                lambda: q[k, 1, 1:9] - deep,
                lambda: deep - q[k, 8, 1:9],
                lambda: q[k, 1:9, 1] - deep,
                lambda: deep - q[k, 1:9, 8],
            ][face]()
            return rf[face, 3] * change

        sx[0] = jnp.sum(far(0), axis=0)
        sx[9] = jnp.sum(far(1), axis=0)
        fy[0] = far(2)
        fy[3] = far(3)

        @pl.loop(0, 8)
        def _(i):
            sum_x = zero
            sum_z = zero
            sum_d = zero
            for j in range(8):
                if base:
                    smoke = dn[i, j]
                    sum_x = sum_x + smoke * vx[i + 1, j]
                    sum_z = sum_z + smoke * vz[i, j]
                    sum_d = sum_d + smoke
                    if j == 0:
                        fy[1, i] = smoke * vy[i, 1]
                    if j == 7:
                        fy[2, i] = smoke * vy[i, 8]
                else:
                    half = hd[i, j]
                    low, high = beside_z(
                        q[k, i + 1, j + 1], zf[2 * k, i, j : j + 1], zf[2 * k + 1, i, j : j + 1]
                    )
                    sum_x = sum_x + half * (q[k, i + 2, j + 1] - q[k, i, j + 1])
                    sum_z = sum_z + half * (high - low)
                    if j == 0:
                        fy[1, i] = half * (q[k, i + 1, 2] - q[k, i + 1, 0])
                    if j == 7:
                        fy[2, i] = half * (q[k, i + 1, 9] - q[k, i + 1, 7])
            sx[i + 1] = sum_x
            sz[i] = sum_z
            if base:
                sd[i] = sum_d
            zt[0, 0, pl.ds(i, 1), :] = sum_z[7:8]
            zt[1, 0, pl.ds(i, 1), :] = sum_z[0:1]

        fy[0] += cube(pick(flat(fy[2]), gl[2]))
        fy[3] += cube(pick(flat(fy[1]), gl[3]))

        def pick_8(x, hot):
            return pick(jnp.concatenate([x, x], axis=0), hot)[:8]

        sx[0] += pick_8(sx[8], gl[0])
        sx[9] += pick_8(sx[1], gl[1])
        z_low = pick_8(zt[0, 0], gl[4])
        z_high = pick_8(zt[1, 0], gl[5])
        for i in range(8):
            low, high = beside_z(sz[i], z_low[i : i + 1], z_high[i : i + 1])
            change = (
                (sx[i + 2] - sx[i])
                + ((fy[3, i] + fy[2, i]) - (fy[1, i] + fy[0, i]))
                + (high - low)
            )
            change = (0.5 * advect_step) * change
            col[8 * i : 8 * i + 8] = marched * (sd[i] - change if base else change)
        columns = parts(col[...])
        total = into_slots(columns[:64]) + into_slots(columns[64:128]) + into_slots(columns[128:])
        das[which] = total.reshape(n_dev, 8, 128)

        @pl.loop(1, n_dev)
        def _(i):
            data_copy(which, i).start()

        dar[which, 0] = das[which, d]

    fill_z_tables(read_z(0))
    local_faces(0)
    apply_local(0)
    take_faces(4)
    for face in range(4):
        smoke_far = cube(pick(rb[4, face], er[face, 0]))
        rf[face, 2] = smoke_far
        rf[face, 3] = 0.5 * smoke_far * rf[face, 0]

    @pl.loop(0, 8)
    def _(i):
        for j in range(8):
            hd[i, j] = 0.5 * dn[i, j] * wp[i + 1, j + 1]

    flux_columns(0)
    take_faces(0)
    add_far(0)
    send_field(1)

    fill_z_tables(read_z(1))
    local_faces(1)
    apply_local(1)
    flux_columns(1)
    m0, m1 = products(0)
    take_faces(1)
    add_far(1)
    send_field(2)

    fill_z_tables(read_z(2))
    local_faces(2)
    apply_local(2)
    flux_columns(2)
    m2, m3 = products(1)
    m4, m5 = products(2)

    take_faces(2)
    far = [cube(pick(rb[2, face], er[face, 0])) for face in range(4)]
    m5_far = zero
    for j in range(8):
        m5_far = m5_far + dg[0, j] * cs[0, 0, j] * far[0][j] * q[2, 1, j + 1]
        m5_far = m5_far + dg[7, j] * cs[1, 7, j] * far[1][j] * q[2, 8, j + 1]
        m5_far = m5_far + dg[j, 0] * cs[2, j, 0] * far[2][j] * q[2, j + 1, 1]
        m5_far = m5_far + dg[j, 7] * cs[3, j, 7] * far[3][j] * q[2, j + 1, 8]

    moments = [m0, m1, m2, m3, m4, m5 - m5_far]
    a1s[...] = jnp.zeros((8, 128), F32)
    for k in range(6):
        line = jnp.sum(moments[k], axis=0, keepdims=True)
        a1s[k : k + 1, :] = line[:, :128] + line[:, 128:]
    for i in range(1, n_grp):
        to_grp(0, a1s, a1r.at[i], i).start()

    q[2, 0, 1:9] += far[0]
    q[2, 9, 1:9] += far[1]
    q[2, 1:9, 0] += far[2]
    q[2, 1:9, 9] += far[3]
    flux_columns(3)

    partial = a1s[...]
    for i in range(1, n_grp):
        to_grp(0, a1s, a1r.at[i], i).wait_recv()
        partial = partial + a1r[i]
    a2s[...] = partial

    @pl.loop(1, n_dev)
    def _(i):
        sum_copy(i).start()

    @pl.loop(1, n_dev)
    def _(i):
        ids_copy(i).wait_recv()

    marks = idr[...].reshape(rows, 128)
    lane_b = lax.broadcasted_iota(jnp.int32, (rows, BLOCKS), 1).astype(F32)
    first_hot = hot_of(marks[:, 0:1] == lane_b)
    second_hot = hot_of(marks[:, 64:65] == lane_b)

    @pl.loop(1, n_dev)
    def _(i):
        ids_copy(i).wait_send()
        for which in range(2):
            data_copy(which, i).wait_send()
            data_copy(which, i).wait_recv()

    @pl.loop(1, n_dev)
    def _(i):
        sum_copy(i).wait_recv()

    whole = partial
    for i in range(1, n_dev):
        whole = whole + a2r[i]
    m = jnp.broadcast_to(jnp.sum(whole, axis=1, keepdims=True), (8, 128))
    m = [m[k : k + 1] for k in range(6)]
    l10 = m[2] / m[1]
    l20 = m[3] / m[1]
    d1 = m[3] - l10 * m[2]
    t21 = m[4] - l20 * m[2]
    l21 = t21 / d1
    d2 = m[5] - l20 * m[3] - l21 * t21
    y1 = m[1] - l10 * m[0]
    y2 = m[2] - l20 * m[0] - l21 * y1
    c2 = y2 / d2
    c1 = y1 / d1 - l21 * c2
    c0 = m[0] / m[1] - l10 * c1 - l20 * c2
    coefs = [jnp.concatenate([spread(c, 8), spread(c, 8)], axis=1) for c in (c0, c1, c2)]

    @pl.loop(1, n_dev)
    def _(i):
        for which in range(2, 4):
            data_copy(which, i).wait_recv()

    columns = dar[0].reshape(rows, 128)
    for k, c in enumerate((c0, c1, c2)):
        columns = columns + spread(c, rows) * dar[k + 1].reshape(rows, 128)
    got = parts(columns.T)
    image = joined(jnp.dot(got, first_hot, preferred_element_type=F32))[:64]
    image = image + joined(jnp.dot(got, second_hot, preferred_element_type=F32))[64:]
    ims[...] = image.reshape(8, 8, BLOCKS)

    def image_copy(i):
        return to_grp(1, ims.at[lax.rem(g + i, n_grp)], imr.at[i], i)

    for i in range(1, n_grp):
        image_copy(i).start()

    def mixed(read):
        return coefs[0] * read(0) + coefs[1] * read(1) + coefs[2] * read(2)

    @pl.loop(0, 8)
    def _(i):
        pp[0, i + 1] = mixed(lambda k: q[k, 0, i + 1])
        pp[9, i + 1] = mixed(lambda k: q[k, 9, i + 1])
        zf[0, i] = mixed(lambda k: zf[2 * k, i])
        zf[1, i] = mixed(lambda k: zf[2 * k + 1, i])
        for j in range(10):
            pp[i + 1, j] = mixed(lambda k: q[k, i + 1, j])

    @pl.loop(0, 8)
    def _(i):
        for j in range(8):
            c = pp[i + 1, j + 1]
            low, high = beside_z(c, zf[0, i, j : j + 1], zf[1, i, j : j + 1])
            half = 0.5 * wp[i + 1, j + 1]
            newv[0, i, j] = vx[i + 1, j] - half * (pp[i + 2, j + 1] - pp[i, j + 1])
            newv[1, i, j] = vy[i, j + 1] - half * (pp[i + 1, j + 2] - pp[i + 1, j])
            newv[2, i, j] = vz[i, j] - half * (high - low)

    for number in range(5):
        for face in range(4):

            @pl.when(sends[face])
            def _():
                halo(number, face).wait_send()

    for i in range(1, n_grp):
        to_grp(0, a1s, a1r.at[i], i).wait_send()

    @pl.loop(1, n_dev)
    def _(i):
        sum_copy(i).wait_send()
        for which in range(2, 4):
            data_copy(which, i).wait_send()

    optical = ims[g]
    for i in range(1, n_grp):
        image_copy(i).wait_recv()
        optical = optical + imr[i]
    shade = 1.0 - jnp.exp(-optical)
    for row in range(8):
        rendered[:, BLOCKS * row : BLOCKS * (row + 1)] = shade[row : row + 1]
    for i in range(1, n_grp):
        image_copy(i).wait_send()


def solution(mesh):
    n_grp, n_dev = mesh.shape["grp"], mesh.shape["dev"]

    def step(
        velocity, density, inverse_density, neighbours, leaf_layer, leaf_tile, leaf_block, samples
    ):
        vmem = pl.BlockSpec(memory_space=pltpu.VMEM)
        anywhere = pl.BlockSpec(memory_space=pl.ANY)
        smem = pl.BlockSpec(memory_space=pltpu.SMEM)
        new_velocity, rendered = pl.pallas_call(
            functools.partial(kernel, n_grp, n_dev),
            out_shape=(
                pltpu.VMEM((3, 8, 8, 8, L), F32),
                pltpu.VMEM((1, 8 * BLOCKS), F32),
            ),
            in_specs=[anywhere] * 7 + [smem],
            out_specs=(vmem, vmem),
            scratch_shapes=[
                pltpu.VMEM((6, L), jnp.int32),
                pltpu.VMEM((3, 1, L), jnp.int32),
                pltpu.VMEM((10, 10, 8, L), F32),
                pltpu.VMEM((10, 8, 8, L), F32),
                pltpu.VMEM((8, 10, 8, L), F32),
                pltpu.VMEM((8, 8, 8, L), F32),
                pltpu.VMEM((8, 8, 8, L), F32),
                pltpu.VMEM((8, 8, 8, L), F32),
                pltpu.VMEM((4, 10, 10, 8, L), F32),
                pltpu.VMEM((6, 8, 8, L), F32),
                pltpu.VMEM((2, 8, 8, L), F32),
                pltpu.VMEM((6, 8, 8, 8, L), F32),
                pltpu.VMEM((8, 8, 8, L), F32),
                pltpu.VMEM((10, 10, 8, L), F32),
                pltpu.VMEM((6, L, L), BF16),
                pltpu.VMEM((4, 2, 2 * FACE, L), BF16),
                pltpu.VMEM((4, 2, 2 * FACE, L), BF16),
                pltpu.VMEM((4, 4, 8, 8, L), F32),
                pltpu.VMEM((5, 4, FACE, 128), F32),
                pltpu.VMEM((5, 4, FACE, 128), F32),
                pltpu.VMEM((8, 128), F32),
                pltpu.VMEM((n_grp, 8, 128), F32),
                pltpu.VMEM((8, 128), F32),
                pltpu.VMEM((n_dev, 8, 128), F32),
                pltpu.VMEM((n_dev, 8, 128), F32),
                pltpu.VMEM((n_dev, 8, 128), F32),
                pltpu.VMEM((4, n_dev, 8, 128), F32),
                pltpu.VMEM((4, n_dev, 8, 128), F32),
                pltpu.VMEM((8, 8, BLOCKS), F32),
                pltpu.VMEM((n_grp, 8, BLOCKS), F32),
                pltpu.VMEM((10, 8, L), F32),
                pltpu.VMEM((4, 8, 8, L), F32),
                pltpu.VMEM((8, 8, L), F32),
                pltpu.VMEM((8, 8, L), F32),
                pltpu.VMEM((64, L), F32),
                pltpu.SemaphoreType.DMA((9,)),
                pltpu.SemaphoreType.DMA((5, 4)),
                pltpu.SemaphoreType.DMA((5, 4)),
                pltpu.SemaphoreType.DMA((2, n_grp)),
                pltpu.SemaphoreType.DMA((2, n_grp)),
                pltpu.SemaphoreType.DMA((6, n_dev)),
                pltpu.SemaphoreType.DMA((6, n_dev)),
            ],
            compiler_params=pltpu.CompilerParams(
                collective_id=0, has_side_effects=True, vmem_limit_bytes=(64 * 1024 - 2048) * 1024
            ),
        )(
            velocity.reshape(3, 8, 8, 8, L),
            density.reshape(8, 8, 8, L),
            inverse_density.reshape(8, 8, 8, L),
            neighbours,
            leaf_layer.reshape(1, L),
            leaf_tile.reshape(1, L),
            leaf_block.reshape(1, L),
            samples,
        )
        return new_velocity.reshape(3, 512, L), rendered

    return jax.shard_map(
        step,
        mesh=mesh,
        in_specs=(
            P(None, None, ("grp", "dev")),
            P(None, ("grp", "dev")),
            P(None, ("grp", "dev")),
            P(None, ("grp", "dev")),
            P(("grp", "dev")),
            P(("grp", "dev"), None),
            P(("grp", "dev")),
            P(),
        ),
        out_specs=(P(None, None, ("grp", "dev")), P("dev", "grp")),
        check_vma=False,
    )
```

time: 74.5 us -> 54.6 us (0.73)
  Pallas kernels: 64.9 us -> 52.1 us
  local copies, waits for them, and re-layouts: 8.61 us -> 1.74 us
    pallas_call x1, Pallas kernels: 64.9 us -> 52.1 us  [step(): pl.pallas_call(functools.partial(kernel, n_grp, n_dev), out_shape=(pltpu....]
    unnamed x18 -> x2, local copies, waits for them, and re-layouts: 8.61 us -> 1.74 us
where the time goes in v2:
time: 54.6 us; the launch traced here: 54.5 us
  Pallas kernels  52.1 us (95%)
  local copies, waits for them, and re-layouts  1.74 us (3%)
  between operations  0.64 us (1%)
    pallas_call x1, Pallas kernels, step(): pl.pallas_call(functools.partial(kernel, n_grp, n_dev), out_shape=(pltpu....  52.1 us
    unnamed x2, local copies, waits for them, and re-layouts  1.74 us

profile of v2, /device:TPU:1, one launch (start us, length us, event | category | flops | bytes accessed | tf_op | source)
XLA Modules:
  0.0 54.5 jit_solution(8867187217302020801)
XLA Ops:
  0.6 52.1 %shard_map.95 = (f32[3,8,8,8,256]{4,3,2,1,0:T(8,128)S(1)}, f32[1,2048]{1,0:T(1,128)S(1)}) custom-call(f32[3,8,8,8,256]{4,3,2,1,0:T(8,128)} %bitcast.8, f32[8,8,8,256]{3,2,1,0:T(8,128)} %bitcast.9, f32[8,8,8,256]{3,2,1,0:T(8,128)} %bitcast.10, s32[6,256]{1,0:T(8,128)} %nbr_any.1, s32[1,256]{1,0:T(1,128)} %bitcast.11, s32[1,256]{1,0:T(1,128)} %bitcast.12, ...), custom_call_target="tpu_custom_call" | custom-call | tf_op jit(solution)/shard_map/pallas_call | solution.py:723
  52.7 1.1 %copy.12 = f32[3,512,256]{2,1,0:T(8,128)} copy(f32[3,512,256]{2,1,0:T(8,128)S(1)} %bitcast.7) | data formatting | bytes 3145728
  53.9 0.6 %copy.13 = f32[1,2048]{1,0:T(1,128)} copy(f32[1,2048]{1,0:T(1,128)S(1)} %get-tuple-element.7) | data formatting | bytes 16384

commit v3 on v2

--- a/solution.py
+++ b/solution.py
@@ -82,6 +82,8 @@
     rf,
     sb,
     rb,
+    sbw,
+    rbw,
     a1s,
     a1r,
     a2s,
@@ -90,6 +92,7 @@
     idr,
     das,
     dar,
+    pix,
     ims,
     imr,
     sx,
@@ -115,6 +118,16 @@
     def dev_at(step):
         return (g, lax.rem(d + step, n_dev))
 
+    barrier = pltpu.get_barrier_semaphore()
+
+    @pl.loop(1, n_grp)
+    def _(i):
+        pl.semaphore_signal(barrier, inc=1, device_id=grp_at(i), device_id_type=MESH)
+
+    @pl.loop(1, n_dev)
+    def _(i):
+        pl.semaphore_signal(barrier, inc=1, device_id=dev_at(i), device_id_type=MESH)
+
     small = [
         pltpu.make_async_copy(nbr_any, nbr, in_sem.at[5]),
         pltpu.make_async_copy(tile_any, rows_in.at[0], in_sem.at[6]),
@@ -139,17 +152,8 @@
 
         @pl.when(jnp.logical_not(takes[face]))
         def _():
-            rb[:, face] = jnp.zeros((5, FACE, 128), F32)
-
-    barrier = pltpu.get_barrier_semaphore()
-
-    @pl.loop(1, n_grp)
-    def _(i):
-        pl.semaphore_signal(barrier, inc=1, device_id=grp_at(i), device_id_type=MESH)
-
-    @pl.loop(1, n_dev)
-    def _(i):
-        pl.semaphore_signal(barrier, inc=1, device_id=dev_at(i), device_id_type=MESH)
+            rb[:, face] = jnp.zeros((7, FACE // 2, 128), F32)
+            rbw[face] = jnp.zeros((FACE, 128), F32)
 
     for load in small:
         load.wait()
@@ -191,25 +195,30 @@
         return x.reshape(8, 8, L)
 
     def halo(number, face):
+        wide = number == 7
         return pltpu.make_async_remote_copy(
-            src_ref=sb.at[number, face],
-            dst_ref=rb.at[number, face],
+            src_ref=sbw.at[face] if wide else sb.at[number, face],
+            dst_ref=rbw.at[face] if wide else rb.at[number, face],
             send_sem=hs_sem.at[number, face],
             recv_sem=hr_sem.at[number, face],
             device_id=to[face],
             device_id_type=MESH,
         )
 
-    def send_faces(number, first, second):
+    def start_faces(number):
         for face in range(4):
-            sb[number, face] = pick_t(flat(first[face]), cp[face, 0]) + pick_t(
-                flat(second[face]), cp[face, 1]
-            )
 
             @pl.when(sends[face])
             def _():
                 halo(number, face).start()
 
+    def pack_faces(number, layers):
+        for face in range(4):
+            rows_64 = flat(layers[face])
+            sb[number, face] = pick_t(rows_64[:32], cp[face, 0]) + pick_t(
+                rows_64[32:], cp[face, 1]
+            )
+
     def take_faces(number):
         for face in range(4):
 
@@ -217,15 +226,23 @@
             def _():
                 halo(number, face).wait_recv()
 
+    def unpacked(number, face):
+        got = parts(rb[number, face])
+        top = joined(jnp.dot(got, er[face, 0], preferred_element_type=F32))
+        bottom = joined(jnp.dot(got, er[face, 1], preferred_element_type=F32))
+        return cube(jnp.concatenate([top, bottom], axis=0))
+
+    first = [wp[8, 1:9], wp[1, 1:9], wp[1:9, 8], wp[1:9, 1]]
+    second = [vx[8], vx[1], vy[:, 8], vy[:, 1]]
+    for face in range(4):
+        sbw[face] = pick_t(flat(first[face]), cp[face, 0]) + pick_t(
+            flat(second[face]), cp[face, 1]
+        )
+
     pl.semaphore_wait(barrier, n_dev - 1 + n_grp - 1)
-
-    send_faces(
-        3,
-        [wp[8, 1:9], wp[1, 1:9], wp[1:9, 8], wp[1:9, 1]],
-        [vx[8], vx[1], vy[:, 8], vy[:, 1]],
-    )
-    smoke_faces = [dn[7], dn[0], dn[:, 7], dn[:, 0]]
-    send_faces(4, smoke_faces, smoke_faces)
+    start_faces(7)
+    pack_faces(6, [dn[7], dn[0], dn[:, 7], dn[:, 0]])
+    start_faces(6)
 
     for face in range(6):
         gl[face] = hot_of(sub == spread(local_slot[face : face + 1], L))
@@ -342,28 +359,6 @@
         both(wp[1:9, 8], vy[:, 8], 2),
         both(wp[1:9, 1], vy[:, 1], 3),
     ]
-    take_faces(3)
-    for face in range(4):
-        got = parts(rb[3, face])
-        w_far = joined(jnp.dot(got, er[face, 0], preferred_element_type=F32))
-        v_far = joined(jnp.dot(got, er[face, 1], preferred_element_type=F32))
-        rf[face, 0] = cube(w_far)
-        rf[face, 1] = cube(v_far)
-        w_near = cube(near_local[face][:FACE] + w_far)
-        v_near = cube(near_local[face][FACE:] + v_far)
-        if face == 0:
-            wp[0, 1:9] = w_near + absent[face] * wp[1, 1:9]
-            vx[0] = v_near
-        elif face == 1:
-            wp[9, 1:9] = w_near + absent[face] * wp[8, 1:9]
-            vx[9] = v_near
-        elif face == 2:
-            wp[1:9, 0] = w_near + absent[face] * wp[1:9, 1]
-            vy[:, 0] = v_near
-        else:
-            wp[1:9, 9] = w_near + absent[face] * wp[1:9, 8]
-            vy[:, 9] = v_near
-
     k_id = lax.broadcasted_iota(jnp.int32, (8, L), 0)
     at_low = k_id == 0
     at_high = k_id == 7
@@ -375,9 +370,8 @@
             jnp.where(at_high, high, pltpu.roll(c, 7, 0)),
         )
 
-    @pl.loop(0, 8)
-    def _(i):
-        for j in range(8):
+    def start(i, columns):
+        for j in columns:
             c = wp[i + 1, j + 1]
             low, high = beside_z(
                 c,
@@ -400,12 +394,46 @@
             )
             q[0, i + 1, j + 1] = source * inverse
 
+    @pl.loop(1, 7)
+    def _(i):
+        start(i, range(1, 7))
+
+    take_faces(7)
+    for face in range(4):
+        got = parts(rbw[face])
+        w_far = joined(jnp.dot(got, er[face, 0], preferred_element_type=F32))
+        v_far = joined(jnp.dot(got, er[face, 1], preferred_element_type=F32))
+        rf[face, 0] = cube(w_far)
+        rf[face, 1] = cube(v_far)
+        w_near = cube(near_local[face][:FACE] + w_far)
+        v_near = cube(near_local[face][FACE:] + v_far)
+        if face == 0:
+            wp[0, 1:9] = w_near + absent[face] * wp[1, 1:9]
+            vx[0] = v_near
+        elif face == 1:
+            wp[9, 1:9] = w_near + absent[face] * wp[8, 1:9]
+            vx[9] = v_near
+        elif face == 2:
+            wp[1:9, 0] = w_near + absent[face] * wp[1:9, 1]
+            vy[:, 0] = v_near
+        else:
+            wp[1:9, 9] = w_near + absent[face] * wp[1:9, 8]
+            vy[:, 9] = v_near
+
+    for i in (0, 7):
+        start(i, range(8))
+
+    @pl.loop(1, 7)
+    def _(i):
+        start(i, (0, 7))
+
     def send_field(k):
-        send_faces(
-            k,
-            [q[k, 8, 1:9], q[k, 1, 1:9], q[k, 1:9, 8], q[k, 1:9, 1]],
-            [q[k, 7, 1:9], q[k, 2, 1:9], q[k, 1:9, 7], q[k, 1:9, 2]],
-        )
+        pack_faces(k, [q[k, 8, 1:9], q[k, 1, 1:9], q[k, 1:9, 8], q[k, 1:9, 1]])
+        start_faces(k)
+
+    def send_deep(k):
+        pack_faces(3 + k, [q[k, 7, 1:9], q[k, 2, 1:9], q[k, 1:9, 7], q[k, 1:9, 2]])
+        start_faces(3 + k)
 
     send_field(0)
 
@@ -429,7 +457,7 @@
                 q[k + 1, i + 1, j + 1] = value
 
     def add_far(k):
-        far = [cube(pick(rb[k, face], er[face, 0])) for face in range(4)]
+        far = [unpacked(k, face) for face in range(4)]
         q[k, 0, 1:9] += far[0]
         q[k, 9, 1:9] += far[1]
         q[k, 1:9, 0] += far[2]
@@ -461,7 +489,7 @@
         def far(face):
             if base:
                 return rf[face, 2] * rf[face, 1]
-            deep = cube(pick(rb[k, face], er[face, 1]))
+            deep = unpacked(3 + k, face)
             change = [
                 lambda: q[k, 1, 1:9] - deep,
                 lambda: deep - q[k, 8, 1:9],
@@ -470,6 +498,8 @@
             ][face]()
             return rf[face, 3] * change
 
+        if not base:
+            take_faces(3 + k)
         sx[0] = jnp.sum(far(0), axis=0)
         sx[9] = jnp.sum(far(1), axis=0)
         fy[0] = far(2)
@@ -537,12 +567,13 @@
 
         dar[which, 0] = das[which, d]
 
+    send_deep(0)
     fill_z_tables(read_z(0))
     local_faces(0)
     apply_local(0)
-    take_faces(4)
+    take_faces(6)
     for face in range(4):
-        smoke_far = cube(pick(rb[4, face], er[face, 0]))
+        smoke_far = unpacked(6, face)
         rf[face, 2] = smoke_far
         rf[face, 3] = 0.5 * smoke_far * rf[face, 0]
 
@@ -556,6 +587,7 @@
     add_far(0)
     send_field(1)
 
+    send_deep(1)
     fill_z_tables(read_z(1))
     local_faces(1)
     apply_local(1)
@@ -565,6 +597,7 @@
     add_far(1)
     send_field(2)
 
+    send_deep(2)
     fill_z_tables(read_z(2))
     local_faces(2)
     apply_local(2)
@@ -573,7 +606,7 @@
     m4, m5 = products(2)
 
     take_faces(2)
-    far = [cube(pick(rb[2, face], er[face, 0])) for face in range(4)]
+    far = [unpacked(2, face) for face in range(4)]
     m5_far = zero
     for j in range(8):
         m5_far = m5_far + dg[0, j] * cs[0, 0, j] * far[0][j] * q[2, 1, j + 1]
@@ -582,10 +615,13 @@
         m5_far = m5_far + dg[j, 7] * cs[3, j, 7] * far[3][j] * q[2, j + 1, 8]
 
     moments = [m0, m1, m2, m3, m4, m5 - m5_far]
-    a1s[...] = jnp.zeros((8, 128), F32)
+    lanes = lax.broadcasted_iota(jnp.int32, (1, 128), 1)
+    row = jnp.zeros((1, 128), F32)
     for k in range(6):
         line = jnp.sum(moments[k], axis=0, keepdims=True)
-        a1s[k : k + 1, :] = line[:, :128] + line[:, 128:]
+        line = jnp.sum(line[:, :128] + line[:, 128:], axis=1, keepdims=True)
+        row = jnp.where(lanes == k, line, row)
+    a1s[...] = row
     for i in range(1, n_grp):
         to_grp(0, a1s, a1r.at[i], i).start()
 
@@ -614,12 +650,26 @@
     first_hot = hot_of(marks[:, 0:1] == lane_b)
     second_hot = hot_of(marks[:, 64:65] == lane_b)
 
+    def pixels(which):
+        got = parts(dar[which].reshape(rows, 128).T)
+        image = joined(jnp.dot(got, first_hot, preferred_element_type=F32))[:64]
+        return image + joined(jnp.dot(got, second_hot, preferred_element_type=F32))[64:]
+
     @pl.loop(1, n_dev)
     def _(i):
         ids_copy(i).wait_send()
-        for which in range(2):
+        for which in range(3):
             data_copy(which, i).wait_send()
             data_copy(which, i).wait_recv()
+
+    for which in range(3):
+        pix[which] = pixels(which)
+
+    @pl.loop(1, n_dev)
+    def _(i):
+        data_copy(3, i).wait_recv()
+
+    pix[3] = pixels(3)
 
     @pl.loop(1, n_dev)
     def _(i):
@@ -628,8 +678,12 @@
     whole = partial
     for i in range(1, n_dev):
         whole = whole + a2r[i]
-    m = jnp.broadcast_to(jnp.sum(whole, axis=1, keepdims=True), (8, 128))
-    m = [m[k : k + 1] for k in range(6)]
+    m = [
+        jnp.broadcast_to(
+            jnp.sum(jnp.where(lanes == k, whole, 0.0), axis=1, keepdims=True), (1, 128)
+        )
+        for k in range(6)
+    ]
     l10 = m[2] / m[1]
     l20 = m[3] / m[1]
     d1 = m[3] - l10 * m[2]
@@ -642,19 +696,11 @@
     c1 = y1 / d1 - l21 * c2
     c0 = m[0] / m[1] - l10 * c1 - l20 * c2
     coefs = [jnp.concatenate([spread(c, 8), spread(c, 8)], axis=1) for c in (c0, c1, c2)]
-
-    @pl.loop(1, n_dev)
-    def _(i):
-        for which in range(2, 4):
-            data_copy(which, i).wait_recv()
-
-    columns = dar[0].reshape(rows, 128)
-    for k, c in enumerate((c0, c1, c2)):
-        columns = columns + spread(c, rows) * dar[k + 1].reshape(rows, 128)
-    got = parts(columns.T)
-    image = joined(jnp.dot(got, first_hot, preferred_element_type=F32))[:64]
-    image = image + joined(jnp.dot(got, second_hot, preferred_element_type=F32))[64:]
-    ims[...] = image.reshape(8, 8, BLOCKS)
+    for row_id in range(8):
+        part = slice(8 * row_id, 8 * row_id + 8)
+        ims[row_id] = (
+            pix[0, part] + coefs[0] * pix[1, part] + coefs[1] * pix[2, part] + coefs[2] * pix[3, part]
+        )
 
     def image_copy(i):
         return to_grp(1, ims.at[lax.rem(g + i, n_grp)], imr.at[i], i)
@@ -684,7 +730,7 @@
             newv[1, i, j] = vy[i, j + 1] - half * (pp[i + 1, j + 2] - pp[i + 1, j])
             newv[2, i, j] = vz[i, j] - half * (high - low)
 
-    for number in range(5):
+    for number in range(8):
         for face in range(4):
 
             @pl.when(sends[face])
@@ -697,8 +743,7 @@
     @pl.loop(1, n_dev)
     def _(i):
         sum_copy(i).wait_send()
-        for which in range(2, 4):
-            data_copy(which, i).wait_send()
+        data_copy(3, i).wait_send()
 
     optical = ims[g]
     for i in range(1, n_grp):
@@ -747,16 +792,19 @@
                 pltpu.VMEM((4, 2, 2 * FACE, L), BF16),
                 pltpu.VMEM((4, 2, 2 * FACE, L), BF16),
                 pltpu.VMEM((4, 4, 8, 8, L), F32),
-                pltpu.VMEM((5, 4, FACE, 128), F32),
-                pltpu.VMEM((5, 4, FACE, 128), F32),
-                pltpu.VMEM((8, 128), F32),
-                pltpu.VMEM((n_grp, 8, 128), F32),
-                pltpu.VMEM((8, 128), F32),
-                pltpu.VMEM((n_dev, 8, 128), F32),
+                pltpu.VMEM((7, 4, FACE // 2, 128), F32),
+                pltpu.VMEM((7, 4, FACE // 2, 128), F32),
+                pltpu.VMEM((4, FACE, 128), F32),
+                pltpu.VMEM((4, FACE, 128), F32),
+                pltpu.VMEM((1, 128), F32),
+                pltpu.VMEM((n_grp, 1, 128), F32),
+                pltpu.VMEM((1, 128), F32),
+                pltpu.VMEM((n_dev, 1, 128), F32),
                 pltpu.VMEM((n_dev, 8, 128), F32),
                 pltpu.VMEM((n_dev, 8, 128), F32),
                 pltpu.VMEM((4, n_dev, 8, 128), F32),
                 pltpu.VMEM((4, n_dev, 8, 128), F32),
+                pltpu.VMEM((4, 64, BLOCKS), F32),
                 pltpu.VMEM((8, 8, BLOCKS), F32),
                 pltpu.VMEM((n_grp, 8, BLOCKS), F32),
                 pltpu.VMEM((10, 8, L), F32),
@@ -765,8 +813,8 @@
                 pltpu.VMEM((8, 8, L), F32),
                 pltpu.VMEM((64, L), F32),
                 pltpu.SemaphoreType.DMA((9,)),
-                pltpu.SemaphoreType.DMA((5, 4)),
-                pltpu.SemaphoreType.DMA((5, 4)),
+                pltpu.SemaphoreType.DMA((8, 4)),
+                pltpu.SemaphoreType.DMA((8, 4)),
                 pltpu.SemaphoreType.DMA((2, n_grp)),
                 pltpu.SemaphoreType.DMA((2, n_grp)),
                 pltpu.SemaphoreType.DMA((6, n_dev)),

time: 54.6 us -> 50.6 us (0.927)
  Pallas kernels: 52.1 us -> 48 us
    pallas_call x1, Pallas kernels: 52.1 us -> 48 us  [step(): pl.pallas_call(functools.partial(kernel, n_grp, n_dev), out_shape=(pltpu....]
where the time goes in v3:
time: 50.6 us; the launch traced here: 50.4 us
  Pallas kernels  48 us (95%)
  local copies, waits for them, and re-layouts  1.74 us (3%)
  between operations  0.64 us (1%)
    pallas_call x1, Pallas kernels, step(): pl.pallas_call(functools.partial(kernel, n_grp, n_dev), out_shape=(pltpu....  48 us
    unnamed x2, local copies, waits for them, and re-layouts  1.74 us

profile of v3, /device:TPU:1, one launch (start us, length us, event | category | flops | bytes accessed | tf_op | source)
XLA Modules:
  0.0 50.4 jit_solution(1763818420537712345)
XLA Ops:
  0.6 48.0 %shard_map.95 = (f32[3,8,8,8,256]{4,3,2,1,0:T(8,128)S(1)}, f32[1,2048]{1,0:T(1,128)S(1)}) custom-call(f32[3,8,8,8,256]{4,3,2,1,0:T(8,128)} %bitcast.8, f32[8,8,8,256]{3,2,1,0:T(8,128)} %bitcast.9, f32[8,8,8,256]{3,2,1,0:T(8,128)} %bitcast.10, s32[6,256]{1,0:T(8,128)} %nbr_any.1, s32[1,256]{1,0:T(1,128)} %bitcast.11, s32[1,256]{1,0:T(1,128)} %bitcast.12, ...), custom_call_target="tpu_custom_call" | custom-call | tf_op jit(solution)/shard_map/pallas_call | solution.py:768
  48.7 1.1 %copy.12 = f32[3,512,256]{2,1,0:T(8,128)} copy(f32[3,512,256]{2,1,0:T(8,128)S(1)} %bitcast.7) | data formatting | bytes 3145728
  49.8 0.6 %copy.13 = f32[1,2048]{1,0:T(1,128)} copy(f32[1,2048]{1,0:T(1,128)S(1)} %get-tuple-element.7) | data formatting | bytes 16384

commit v4 on v3

--- a/solution.py
+++ b/solution.py
@@ -93,7 +93,6 @@
     das,
     dar,
     pix,
-    ims,
     imr,
     sx,
     fy,
@@ -107,6 +106,7 @@
     gr_sem,
     ds_sem,
     dr_sem,
+    relay_sem,
 ):
     g = lax.axis_index("grp")
     d = lax.axis_index("dev")
@@ -118,15 +118,24 @@
     def dev_at(step):
         return (g, lax.rem(d + step, n_dev))
 
+    def torus_at(step_x, step_z):
+        x = lax.rem(d // 8 + step_x, n_dev // 8)
+        return (g, x * 8 + lax.rem(lax.rem(d, 8) + step_z, 8))
+
+    two_away = [torus_at(0, 2), torus_at(0, 6), torus_at(2, 0)] + [
+        torus_at(x, z) for x in (1, n_dev // 8 - 1) for z in (1, 7)
+    ]
+    greeted = [torus_at(0, 1), torus_at(0, 7), torus_at(1, 0), torus_at(n_dev // 8 - 1, 0)]
+    greeted = [grp_at(i) for i in range(1, n_grp)] + greeted + two_away
     barrier = pltpu.get_barrier_semaphore()
-
-    @pl.loop(1, n_grp)
-    def _(i):
-        pl.semaphore_signal(barrier, inc=1, device_id=grp_at(i), device_id_type=MESH)
-
-    @pl.loop(1, n_dev)
-    def _(i):
-        pl.semaphore_signal(barrier, inc=1, device_id=dev_at(i), device_id_type=MESH)
+    for who in greeted:
+        pl.semaphore_signal(barrier, inc=1, device_id=who, device_id_type=MESH)
+
+    def relay(number):
+        for who in two_away:
+            pl.semaphore_signal(
+                relay_sem.at[number], inc=1, device_id=who, device_id_type=MESH
+            )
 
     small = [
         pltpu.make_async_copy(nbr_any, nbr, in_sem.at[5]),
@@ -239,8 +248,9 @@
             flat(second[face]), cp[face, 1]
         )
 
-    pl.semaphore_wait(barrier, n_dev - 1 + n_grp - 1)
+    pl.semaphore_wait(barrier, len(greeted))
     start_faces(7)
+    relay(0)
     pack_faces(6, [dn[7], dn[0], dn[:, 7], dn[:, 0]])
     start_faces(6)
 
@@ -312,11 +322,19 @@
     def data_copy(which, i):
         return to_dev(2 + which, das.at[which, lax.rem(d + i, n_dev)], dar.at[which, i], i)
 
-    ids[...] = into_slots(spread(rows_in[1], 64).astype(F32).astype(BF16)).reshape(n_dev, 8, 128)
-
-    @pl.loop(1, n_dev)
-    def _(i):
-        ids_copy(i).start()
+    marked = jnp.where(
+        lax.broadcasted_iota(jnp.int32, (128, L), 0) == spread(rank, 128),
+        spread(rows_in[1], 128),
+        0,
+    )
+    marked = lax.dot_general(
+        tile_hot,
+        marked.astype(F32).astype(BF16),
+        (((1,), (1,)), ((), ())),
+        preferred_element_type=F32,
+    )
+    for t in range(n_dev):
+        ids[t] = marked[t : t + 1]
 
     idr[0] = ids[d]
     limit = jnp.zeros((1, L), jnp.int32)
@@ -399,6 +417,8 @@
         start(i, range(1, 7))
 
     take_faces(7)
+    pl.semaphore_wait(relay_sem.at[0], len(two_away))
+    relay(1)
     for face in range(4):
         got = parts(rbw[face])
         w_far = joined(jnp.dot(got, er[face, 0], preferred_element_type=F32))
@@ -482,28 +502,9 @@
     def read_z(k):
         return lambda i, j: q[k, i + 1, j + 1]
 
-    def flux_columns(which):
+    def flux_local(which):
         base = which == 0
         k = which - 1
-
-        def far(face):
-            if base:
-                return rf[face, 2] * rf[face, 1]
-            deep = unpacked(3 + k, face)
-            change = [
-                lambda: q[k, 1, 1:9] - deep,
-                lambda: deep - q[k, 8, 1:9],
-                lambda: q[k, 1:9, 1] - deep,
-                lambda: deep - q[k, 1:9, 8],
-            ][face]()
-            return rf[face, 3] * change
-
-        if not base:
-            take_faces(3 + k)
-        sx[0] = jnp.sum(far(0), axis=0)
-        sx[9] = jnp.sum(far(1), axis=0)
-        fy[0] = far(2)
-        fy[3] = far(3)
 
         @pl.loop(0, 8)
         def _(i):
@@ -538,6 +539,29 @@
             zt[0, 0, pl.ds(i, 1), :] = sum_z[7:8]
             zt[1, 0, pl.ds(i, 1), :] = sum_z[0:1]
 
+    def flux_finish(which):
+        base = which == 0
+        k = which - 1
+
+        def far(face):
+            if base:
+                return rf[face, 2] * rf[face, 1]
+            deep = unpacked(3 + k, face)
+            change = [
+                lambda: q[k, 1, 1:9] - deep,
+                lambda: deep - q[k, 8, 1:9],
+                lambda: q[k, 1:9, 1] - deep,
+                lambda: deep - q[k, 1:9, 8],
+            ][face]()
+            return rf[face, 3] * change
+
+        if not base:
+            take_faces(3 + k)
+        sx[0] = jnp.sum(far(0), axis=0)
+        sx[9] = jnp.sum(far(1), axis=0)
+        fy[0] = far(2)
+        fy[3] = far(3)
+
         fy[0] += cube(pick(flat(fy[2]), gl[2]))
         fy[3] += cube(pick(flat(fy[1]), gl[3]))
 
@@ -560,12 +584,16 @@
         columns = parts(col[...])
         total = into_slots(columns[:64]) + into_slots(columns[64:128]) + into_slots(columns[128:])
         das[which] = total.reshape(n_dev, 8, 128)
-
+        dar[which, 0] = das[which, d]
+
+    def send_columns(which):
         @pl.loop(1, n_dev)
         def _(i):
             data_copy(which, i).start()
 
-        dar[which, 0] = das[which, d]
+    def flux_columns(which):
+        flux_local(which)
+        flux_finish(which)
 
     send_deep(0)
     fill_z_tables(read_z(0))
@@ -583,6 +611,13 @@
             hd[i, j] = 0.5 * dn[i, j] * wp[i + 1, j + 1]
 
     flux_columns(0)
+    pl.semaphore_wait(relay_sem.at[1], len(two_away))
+
+    @pl.loop(1, n_dev)
+    def _(i):
+        ids_copy(i).start()
+
+    send_columns(0)
     take_faces(0)
     add_far(0)
     send_field(1)
@@ -592,6 +627,7 @@
     local_faces(1)
     apply_local(1)
     flux_columns(1)
+    send_columns(1)
     m0, m1 = products(0)
     take_faces(1)
     add_far(1)
@@ -602,8 +638,10 @@
     local_faces(2)
     apply_local(2)
     flux_columns(2)
+    send_columns(2)
     m2, m3 = products(1)
     m4, m5 = products(2)
+    flux_local(3)
 
     take_faces(2)
     far = [unpacked(2, face) for face in range(4)]
@@ -629,7 +667,13 @@
     q[2, 9, 1:9] += far[1]
     q[2, 1:9, 0] += far[2]
     q[2, 1:9, 9] += far[3]
-    flux_columns(3)
+    for j in range(8):
+        sx[1] -= hd[0, j] * far[0][j]
+        sx[8] += hd[7, j] * far[1][j]
+        fy[1, j] -= hd[j, 0] * far[2][j]
+        fy[2, j] += hd[j, 7] * far[3][j]
+    flux_finish(3)
+    send_columns(3)
 
     partial = a1s[...]
     for i in range(1, n_grp):
@@ -645,15 +689,27 @@
     def _(i):
         ids_copy(i).wait_recv()
 
-    marks = idr[...].reshape(rows, 128)
+    marks = jnp.concatenate([spread(idr[i], 8) for i in range(n_dev)], axis=0)
+    mark_lane = lax.broadcasted_iota(jnp.int32, (rows, 128), 1)
+    mark_row = lax.broadcasted_iota(jnp.int32, (rows, 128), 0) % 8
+    first_mark = jnp.sum(jnp.where(mark_lane == mark_row, marks, 0.0), axis=1, keepdims=True)
+    second_mark = jnp.sum(
+        jnp.where(mark_lane == mark_row + 8, marks, 0.0), axis=1, keepdims=True
+    )
     lane_b = lax.broadcasted_iota(jnp.int32, (rows, BLOCKS), 1).astype(F32)
-    first_hot = hot_of(marks[:, 0:1] == lane_b)
-    second_hot = hot_of(marks[:, 64:65] == lane_b)
-
-    def pixels(which):
+    first_hot = hot_of(first_mark == lane_b)
+    second_hot = hot_of(second_mark == lane_b)
+
+    def image_copy(which, i):
+        return to_grp(1 + which, pix.at[which, lax.rem(g + i, n_grp)], imr.at[which, i], i)
+
+    def send_pixels(which):
         got = parts(dar[which].reshape(rows, 128).T)
         image = joined(jnp.dot(got, first_hot, preferred_element_type=F32))[:64]
-        return image + joined(jnp.dot(got, second_hot, preferred_element_type=F32))[64:]
+        image = image + joined(jnp.dot(got, second_hot, preferred_element_type=F32))[64:]
+        pix[which] = image.reshape(8, 8, BLOCKS)
+        for i in range(1, n_grp):
+            image_copy(which, i).start()
 
     @pl.loop(1, n_dev)
     def _(i):
@@ -663,13 +719,13 @@
             data_copy(which, i).wait_recv()
 
     for which in range(3):
-        pix[which] = pixels(which)
+        send_pixels(which)
 
     @pl.loop(1, n_dev)
     def _(i):
         data_copy(3, i).wait_recv()
 
-    pix[3] = pixels(3)
+    send_pixels(3)
 
     @pl.loop(1, n_dev)
     def _(i):
@@ -696,18 +752,6 @@
     c1 = y1 / d1 - l21 * c2
     c0 = m[0] / m[1] - l10 * c1 - l20 * c2
     coefs = [jnp.concatenate([spread(c, 8), spread(c, 8)], axis=1) for c in (c0, c1, c2)]
-    for row_id in range(8):
-        part = slice(8 * row_id, 8 * row_id + 8)
-        ims[row_id] = (
-            pix[0, part] + coefs[0] * pix[1, part] + coefs[1] * pix[2, part] + coefs[2] * pix[3, part]
-        )
-
-    def image_copy(i):
-        return to_grp(1, ims.at[lax.rem(g + i, n_grp)], imr.at[i], i)
-
-    for i in range(1, n_grp):
-        image_copy(i).start()
-
     def mixed(read):
         return coefs[0] * read(0) + coefs[1] * read(1) + coefs[2] * read(2)
 
@@ -745,15 +789,19 @@
         sum_copy(i).wait_send()
         data_copy(3, i).wait_send()
 
-    optical = ims[g]
-    for i in range(1, n_grp):
-        image_copy(i).wait_recv()
-        optical = optical + imr[i]
+    optical = zero
+    for which in range(4):
+        layer_sum = pix[which, g]
+        for i in range(1, n_grp):
+            image_copy(which, i).wait_recv()
+            layer_sum = layer_sum + imr[which, i]
+        optical = optical + (layer_sum if which == 0 else coefs[which - 1] * layer_sum)
     shade = 1.0 - jnp.exp(-optical)
     for row in range(8):
         rendered[:, BLOCKS * row : BLOCKS * (row + 1)] = shade[row : row + 1]
-    for i in range(1, n_grp):
-        image_copy(i).wait_send()
+    for which in range(4):
+        for i in range(1, n_grp):
+            image_copy(which, i).wait_send()
 
 
 def solution(mesh):
@@ -800,13 +848,12 @@
                 pltpu.VMEM((n_grp, 1, 128), F32),
                 pltpu.VMEM((1, 128), F32),
                 pltpu.VMEM((n_dev, 1, 128), F32),
-                pltpu.VMEM((n_dev, 8, 128), F32),
-                pltpu.VMEM((n_dev, 8, 128), F32),
+                pltpu.VMEM((n_dev, 1, 128), F32),
+                pltpu.VMEM((n_dev, 1, 128), F32),
                 pltpu.VMEM((4, n_dev, 8, 128), F32),
                 pltpu.VMEM((4, n_dev, 8, 128), F32),
-                pltpu.VMEM((4, 64, BLOCKS), F32),
-                pltpu.VMEM((8, 8, BLOCKS), F32),
-                pltpu.VMEM((n_grp, 8, BLOCKS), F32),
+                pltpu.VMEM((4, 8, 8, BLOCKS), F32),
+                pltpu.VMEM((4, n_grp, 8, BLOCKS), F32),
                 pltpu.VMEM((10, 8, L), F32),
                 pltpu.VMEM((4, 8, 8, L), F32),
                 pltpu.VMEM((8, 8, L), F32),
@@ -815,10 +862,11 @@
                 pltpu.SemaphoreType.DMA((9,)),
                 pltpu.SemaphoreType.DMA((8, 4)),
                 pltpu.SemaphoreType.DMA((8, 4)),
-                pltpu.SemaphoreType.DMA((2, n_grp)),
-                pltpu.SemaphoreType.DMA((2, n_grp)),
+                pltpu.SemaphoreType.DMA((5, n_grp)),
+                pltpu.SemaphoreType.DMA((5, n_grp)),
                 pltpu.SemaphoreType.DMA((6, n_dev)),
                 pltpu.SemaphoreType.DMA((6, n_dev)),
+                pltpu.SemaphoreType.REGULAR((2,)),
             ],
             compiler_params=pltpu.CompilerParams(
                 collective_id=0, has_side_effects=True, vmem_limit_bytes=(64 * 1024 - 2048) * 1024

time: 50.6 us -> 48 us (0.949)
  Pallas kernels: 48 us -> 45.5 us
    pallas_call x1, Pallas kernels: 48 us -> 45.5 us  [step(): pl.pallas_call(functools.partial(kernel, n_grp, n_dev), out_shape=(pltpu....]
where the time goes in v4:
time: 48 us; the launch traced here: 47.9 us
  Pallas kernels  45.5 us (95%)
  local copies, waits for them, and re-layouts  1.74 us (4%)
  between operations  0.64 us (1%)
    pallas_call x1, Pallas kernels, step(): pl.pallas_call(functools.partial(kernel, n_grp, n_dev), out_shape=(pltpu....  45.5 us
    unnamed x2, local copies, waits for them, and re-layouts  1.74 us

profile of v4, /device:TPU:1, one launch (start us, length us, event | category | flops | bytes accessed | tf_op | source)
XLA Modules:
  0.0 47.9 jit_solution(12197908020511654021)
XLA Ops:
  0.6 45.5 %shard_map.95 = (f32[3,8,8,8,256]{4,3,2,1,0:T(8,128)S(1)}, f32[1,2048]{1,0:T(1,128)S(1)}) custom-call(f32[3,8,8,8,256]{4,3,2,1,0:T(8,128)} %bitcast.8, f32[8,8,8,256]{3,2,1,0:T(8,128)} %bitcast.9, f32[8,8,8,256]{3,2,1,0:T(8,128)} %bitcast.10, s32[6,256]{1,0:T(8,128)} %nbr_any.1, s32[1,256]{1,0:T(1,128)} %bitcast.11, s32[1,256]{1,0:T(1,128)} %bitcast.12, ...), custom_call_target="tpu_custom_call" | custom-call | tf_op jit(solution)/shard_map/pallas_call | solution.py:816
  46.1 1.1 %copy.12 = f32[3,512,256]{2,1,0:T(8,128)} copy(f32[3,512,256]{2,1,0:T(8,128)S(1)} %bitcast.7) | data formatting | bytes 3145728
  47.3 0.6 %copy.13 = f32[1,2048]{1,0:T(1,128)} copy(f32[1,2048]{1,0:T(1,128)S(1)} %get-tuple-element.7) | data formatting | bytes 16384

commit v5 on v4

--- a/solution.py
+++ b/solution.py
@@ -297,8 +297,8 @@
         return pltpu.make_async_remote_copy(
             src_ref=src,
             dst_ref=dst,
-            send_sem=ds_sem.at[number, i],
-            recv_sem=dr_sem.at[number, i],
+            send_sem=ds_sem.at[number],
+            recv_sem=dr_sem.at[number],
             device_id=dev_at(i),
             device_id_type=MESH,
         )
@@ -307,11 +307,21 @@
         return pltpu.make_async_remote_copy(
             src_ref=src,
             dst_ref=dst,
-            send_sem=gs_sem.at[number, i],
-            recv_sem=gr_sem.at[number, i],
+            send_sem=gs_sem.at[number],
+            recv_sem=gr_sem.at[number],
             device_id=grp_at(i),
             device_id_type=MESH,
         )
+
+    def all_dev(number):
+        got = [idr, a2r, dar.at[0], dar.at[1], dar.at[2], dar.at[3]][number]
+        got = got.at[pl.ds(1, n_dev - 1)]
+        return to_dev(number, got, got, 1)
+
+    def all_grp(number):
+        got = [a1r, imr.at[0], imr.at[1], imr.at[2], imr.at[3]][number]
+        got = got.at[pl.ds(1, n_grp - 1)]
+        return to_grp(number, got, got, 1)
 
     def ids_copy(i):
         return to_dev(0, ids.at[lax.rem(d + i, n_dev)], idr.at[i], i)
@@ -539,6 +549,19 @@
             zt[0, 0, pl.ds(i, 1), :] = sum_z[7:8]
             zt[1, 0, pl.ds(i, 1), :] = sum_z[0:1]
 
+        def pick_8(x, hot):
+            return pick(jnp.concatenate([x, x], axis=0), hot)[:8]
+
+        sx[0] = pick_8(sx[8], gl[0])
+        sx[9] = pick_8(sx[1], gl[1])
+        fy[0] = cube(pick(flat(fy[2]), gl[2]))
+        fy[3] = cube(pick(flat(fy[1]), gl[3]))
+        z_low = pick_8(zt[0, 0], gl[4])
+        z_high = pick_8(zt[1, 0], gl[5])
+        for i in range(8):
+            low, high = beside_z(sz[i], z_low[i : i + 1], z_high[i : i + 1])
+            sz[i] = high - low
+
     def flux_finish(which):
         base = which == 0
         k = which - 1
@@ -557,27 +580,16 @@
 
         if not base:
             take_faces(3 + k)
-        sx[0] = jnp.sum(far(0), axis=0)
-        sx[9] = jnp.sum(far(1), axis=0)
-        fy[0] = far(2)
-        fy[3] = far(3)
-
-        fy[0] += cube(pick(flat(fy[2]), gl[2]))
-        fy[3] += cube(pick(flat(fy[1]), gl[3]))
-
-        def pick_8(x, hot):
-            return pick(jnp.concatenate([x, x], axis=0), hot)[:8]
-
-        sx[0] += pick_8(sx[8], gl[0])
-        sx[9] += pick_8(sx[1], gl[1])
-        z_low = pick_8(zt[0, 0], gl[4])
-        z_high = pick_8(zt[1, 0], gl[5])
+        sx[0] += jnp.sum(far(0), axis=0)
+        sx[9] += jnp.sum(far(1), axis=0)
+        fy[0] += far(2)
+        fy[3] += far(3)
+
         for i in range(8):
-            low, high = beside_z(sz[i], z_low[i : i + 1], z_high[i : i + 1])
             change = (
                 (sx[i + 2] - sx[i])
                 + ((fy[3, i] + fy[2, i]) - (fy[1, i] + fy[0, i]))
-                + (high - low)
+                + sz[i]
             )
             change = (0.5 * advect_step) * change
             col[8 * i : 8 * i + 8] = marched * (sd[i] - change if base else change)
@@ -623,28 +635,36 @@
     send_field(1)
 
     send_deep(1)
+    flux_columns(1)
+    send_columns(1)
     fill_z_tables(read_z(1))
     local_faces(1)
     apply_local(1)
-    flux_columns(1)
-    send_columns(1)
     m0, m1 = products(0)
     take_faces(1)
     add_far(1)
     send_field(2)
 
     send_deep(2)
+    flux_columns(2)
+    send_columns(2)
     fill_z_tables(read_z(2))
     local_faces(2)
     apply_local(2)
-    flux_columns(2)
-    send_columns(2)
     m2, m3 = products(1)
     m4, m5 = products(2)
     flux_local(3)
 
     take_faces(2)
     far = [unpacked(2, face) for face in range(4)]
+    for j in range(8):
+        sx[1] -= hd[0, j] * far[0][j]
+        sx[8] += hd[7, j] * far[1][j]
+        fy[1, j] -= hd[j, 0] * far[2][j]
+        fy[2, j] += hd[j, 7] * far[3][j]
+    flux_finish(3)
+    send_columns(3)
+
     m5_far = zero
     for j in range(8):
         m5_far = m5_far + dg[0, j] * cs[0, 0, j] * far[0][j] * q[2, 1, j + 1]
@@ -667,17 +687,9 @@
     q[2, 9, 1:9] += far[1]
     q[2, 1:9, 0] += far[2]
     q[2, 1:9, 9] += far[3]
-    for j in range(8):
-        sx[1] -= hd[0, j] * far[0][j]
-        sx[8] += hd[7, j] * far[1][j]
-        fy[1, j] -= hd[j, 0] * far[2][j]
-        fy[2, j] += hd[j, 7] * far[3][j]
-    flux_finish(3)
-    send_columns(3)
-
     partial = a1s[...]
+    all_grp(0).wait_recv()
     for i in range(1, n_grp):
-        to_grp(0, a1s, a1r.at[i], i).wait_recv()
         partial = partial + a1r[i]
     a2s[...] = partial
 
@@ -685,9 +697,7 @@
     def _(i):
         sum_copy(i).start()
 
-    @pl.loop(1, n_dev)
-    def _(i):
-        ids_copy(i).wait_recv()
+    all_dev(0).wait_recv()
 
     marks = jnp.concatenate([spread(idr[i], 8) for i in range(n_dev)], axis=0)
     mark_lane = lax.broadcasted_iota(jnp.int32, (rows, 128), 1)
@@ -711,25 +721,15 @@
         for i in range(1, n_grp):
             image_copy(which, i).start()
 
-    @pl.loop(1, n_dev)
-    def _(i):
-        ids_copy(i).wait_send()
-        for which in range(3):
-            data_copy(which, i).wait_send()
-            data_copy(which, i).wait_recv()
-
     for which in range(3):
+        all_dev(2 + which).wait_recv()
         send_pixels(which)
 
-    @pl.loop(1, n_dev)
-    def _(i):
-        data_copy(3, i).wait_recv()
+    all_dev(5).wait_recv()
 
     send_pixels(3)
 
-    @pl.loop(1, n_dev)
-    def _(i):
-        sum_copy(i).wait_recv()
+    all_dev(1).wait_recv()
 
     whole = partial
     for i in range(1, n_dev):
@@ -781,27 +781,23 @@
             def _():
                 halo(number, face).wait_send()
 
-    for i in range(1, n_grp):
-        to_grp(0, a1s, a1r.at[i], i).wait_send()
-
-    @pl.loop(1, n_dev)
-    def _(i):
-        sum_copy(i).wait_send()
-        data_copy(3, i).wait_send()
+    all_grp(0).wait_send()
+
+    for number in range(6):
+        all_dev(number).wait_send()
 
     optical = zero
     for which in range(4):
         layer_sum = pix[which, g]
+        all_grp(1 + which).wait_recv()
         for i in range(1, n_grp):
-            image_copy(which, i).wait_recv()
             layer_sum = layer_sum + imr[which, i]
         optical = optical + (layer_sum if which == 0 else coefs[which - 1] * layer_sum)
     shade = 1.0 - jnp.exp(-optical)
     for row in range(8):
         rendered[:, BLOCKS * row : BLOCKS * (row + 1)] = shade[row : row + 1]
     for which in range(4):
-        for i in range(1, n_grp):
-            image_copy(which, i).wait_send()
+        all_grp(1 + which).wait_send()
 
 
 def solution(mesh):
@@ -862,10 +858,10 @@
                 pltpu.SemaphoreType.DMA((9,)),
                 pltpu.SemaphoreType.DMA((8, 4)),
                 pltpu.SemaphoreType.DMA((8, 4)),
-                pltpu.SemaphoreType.DMA((5, n_grp)),
-                pltpu.SemaphoreType.DMA((5, n_grp)),
-                pltpu.SemaphoreType.DMA((6, n_dev)),
-                pltpu.SemaphoreType.DMA((6, n_dev)),
+                pltpu.SemaphoreType.DMA((5,)),
+                pltpu.SemaphoreType.DMA((5,)),
+                pltpu.SemaphoreType.DMA((6,)),
+                pltpu.SemaphoreType.DMA((6,)),
                 pltpu.SemaphoreType.REGULAR((2,)),
             ],
             compiler_params=pltpu.CompilerParams(

time: 48 us -> 43.7 us (0.910)
  Pallas kernels: 45.5 us -> 41.2 us
    pallas_call x1, Pallas kernels: 45.5 us -> 41.2 us  [step(): pl.pallas_call(functools.partial(kernel, n_grp, n_dev), out_shape=(pltpu....]
where the time goes in v5:
time: 43.7 us; the launch traced here: 43.6 us
  Pallas kernels  41.2 us (94%)
  local copies, waits for them, and re-layouts  1.74 us (4%)
  between operations  0.64 us (1%)
    pallas_call x1, Pallas kernels, step(): pl.pallas_call(functools.partial(kernel, n_grp, n_dev), out_shape=(pltpu....  41.2 us
    unnamed x2, local copies, waits for them, and re-layouts  1.74 us

profile of v5, /device:TPU:1, one launch (start us, length us, event | category | flops | bytes accessed | tf_op | source)
XLA Modules:
  0.0 43.6 jit_solution(5052288461306906311)
XLA Ops:
  0.6 41.2 %shard_map.95 = (f32[3,8,8,8,256]{4,3,2,1,0:T(8,128)S(1)}, f32[1,2048]{1,0:T(1,128)S(1)}) custom-call(f32[3,8,8,8,256]{4,3,2,1,0:T(8,128)} %bitcast.8, f32[8,8,8,256]{3,2,1,0:T(8,128)} %bitcast.9, f32[8,8,8,256]{3,2,1,0:T(8,128)} %bitcast.10, s32[6,256]{1,0:T(8,128)} %nbr_any.1, s32[1,256]{1,0:T(1,128)} %bitcast.11, s32[1,256]{1,0:T(1,128)} %bitcast.12, ...), custom_call_target="tpu_custom_call" | custom-call | tf_op jit(solution)/shard_map/pallas_call | solution.py:812
  41.9 1.1 %copy.12 = f32[3,512,256]{2,1,0:T(8,128)} copy(f32[3,512,256]{2,1,0:T(8,128)S(1)} %bitcast.7) | data formatting | bytes 3145728
  43.0 0.6 %copy.13 = f32[1,2048]{1,0:T(1,128)} copy(f32[1,2048]{1,0:T(1,128)S(1)} %get-tuple-element.7) | data formatting | bytes 16384

commit v6 on v5

--- a/solution.py
+++ b/solution.py
@@ -208,7 +208,7 @@
         return pltpu.make_async_remote_copy(
             src_ref=sbw.at[face] if wide else sb.at[number, face],
             dst_ref=rbw.at[face] if wide else rb.at[number, face],
-            send_sem=hs_sem.at[number, face],
+            send_sem=hs_sem.at[1 if wide else 0, face],
             recv_sem=hr_sem.at[number, face],
             device_id=to[face],
             device_id_type=MESH,
@@ -599,7 +599,7 @@
         dar[which, 0] = das[which, d]
 
     def send_columns(which):
-        @pl.loop(1, n_dev)
+        @pl.loop(1, n_dev, unroll=True)
         def _(i):
             data_copy(which, i).start()
 
@@ -625,7 +625,7 @@
     flux_columns(0)
     pl.semaphore_wait(relay_sem.at[1], len(two_away))
 
-    @pl.loop(1, n_dev)
+    @pl.loop(1, n_dev, unroll=True)
     def _(i):
         ids_copy(i).start()
 
@@ -693,7 +693,7 @@
         partial = partial + a1r[i]
     a2s[...] = partial
 
-    @pl.loop(1, n_dev)
+    @pl.loop(1, n_dev, unroll=True)
     def _(i):
         sum_copy(i).start()
 
@@ -774,12 +774,19 @@
             newv[1, i, j] = vy[i, j + 1] - half * (pp[i + 1, j + 2] - pp[i + 1, j])
             newv[2, i, j] = vz[i, j] - half * (high - low)
 
-    for number in range(8):
-        for face in range(4):
-
-            @pl.when(sends[face])
-            def _():
-                halo(number, face).wait_send()
+    for face in range(4):
+
+        @pl.when(sends[face])
+        def _():
+            halo(7, face).wait_send()
+            pltpu.make_async_remote_copy(
+                src_ref=sb.at[:, face],
+                dst_ref=rb.at[:, face],
+                send_sem=hs_sem.at[0, face],
+                recv_sem=hr_sem.at[0, face],
+                device_id=to[face],
+                device_id_type=MESH,
+            ).wait_send()
 
     all_grp(0).wait_send()
 
@@ -856,7 +863,7 @@
                 pltpu.VMEM((8, 8, L), F32),
                 pltpu.VMEM((64, L), F32),
                 pltpu.SemaphoreType.DMA((9,)),
-                pltpu.SemaphoreType.DMA((8, 4)),
+                pltpu.SemaphoreType.DMA((2, 4)),
                 pltpu.SemaphoreType.DMA((8, 4)),
                 pltpu.SemaphoreType.DMA((5,)),
                 pltpu.SemaphoreType.DMA((5,)),

time: 43.7 us -> 43.2 us (0.989)
  Pallas kernels: 41.2 us -> 40.7 us
    pallas_call x1, Pallas kernels: 41.2 us -> 40.7 us  [step(): pl.pallas_call(functools.partial(kernel, n_grp, n_dev), out_shape=(pltpu....]
where the time goes in v6:
time: 43.2 us; the launch traced here: 43.1 us
  Pallas kernels  40.7 us (94%)
  local copies, waits for them, and re-layouts  1.74 us (4%)
  between operations  0.64 us (1%)
    pallas_call x1, Pallas kernels, step(): pl.pallas_call(functools.partial(kernel, n_grp, n_dev), out_shape=(pltpu....  40.7 us
    unnamed x2, local copies, waits for them, and re-layouts  1.74 us

profile of v6, /device:TPU:1, one launch (start us, length us, event | category | flops | bytes accessed | tf_op | source)
XLA Modules:
  0.0 43.1 jit_solution(12844979889878104708)
XLA Ops:
  0.6 40.7 %shard_map.95 = (f32[3,8,8,8,256]{4,3,2,1,0:T(8,128)S(1)}, f32[1,2048]{1,0:T(1,128)S(1)}) custom-call(f32[3,8,8,8,256]{4,3,2,1,0:T(8,128)} %bitcast.8, f32[8,8,8,256]{3,2,1,0:T(8,128)} %bitcast.9, f32[8,8,8,256]{3,2,1,0:T(8,128)} %bitcast.10, s32[6,256]{1,0:T(8,128)} %nbr_any.1, s32[1,256]{1,0:T(1,128)} %bitcast.11, s32[1,256]{1,0:T(1,128)} %bitcast.12, ...), custom_call_target="tpu_custom_call" | custom-call | tf_op jit(solution)/shard_map/pallas_call | solution.py:819
  41.4 1.1 %copy.12 = f32[3,512,256]{2,1,0:T(8,128)} copy(f32[3,512,256]{2,1,0:T(8,128)S(1)} %bitcast.7) | data formatting | bytes 3145728
  42.5 0.6 %copy.13 = f32[1,2048]{1,0:T(1,128)} copy(f32[1,2048]{1,0:T(1,128)S(1)} %get-tuple-element.7) | data formatting | bytes 16384
